TPU v7x, 128 devices: a whole 4x4x4 slice. The times are simulated.
128 devices in a mesh: blk: 16 (over z_hi, y, core), pair: 8 (over x, z_lo).
Axes of the slice: x: 4, y: 4, z: 4 (z_hi: 2, z_lo: 2; z = z_hi * 2 + z_lo), core: 2. Of those that a mesh axis runs over, the one named last changes fastest.
Arguments:
- density: float32 [160, 512, 256], P('pair', 'blk'), may hold values from 0.05 to 2
- agg_kernel: float32 [160, 160], replicated, may hold values from 0.00125 to 0.0125
- pair_share: float32 [160, 160], replicated, may hold values from 0 to 1
- pair_target: int32 [160, 160], replicated, may hold values from 0 to 158, as said below
- fragments: float32 [160, 160], replicated, may hold values from 0 to 0.025
- break_rate: float32 [160], replicated, may hold values from 0.05 to 0.4
- courant: float32 [160], replicated, may hold values from 0.2 to 0.9
- block_rows: int32 [16], replicated, may hold values from 1 to 32, 384 in all
- upstream: int32 [16], replicated, may hold values from 0 to 15, as said below
- face_map: int32 [16, 256], P('blk'), may hold values from 0 to 255, each once within a row
Outputs:
- updated: float32 [160, 512, 256], P('pair', 'blk')
Inputs may be any that keep to these rules, and one draw needn't show every extreme that they name: `pair_target`: entry (i, j) lies from min(max(i, j), 158) to min(max(i, j) + 3, 158). `upstream`: the links form one cycle through all 16 blocks: every block feeds exactly one block and none feeds itself.
All inputs are finite; a program needn't handle non-finite values.
Results may differ from a plain program's by a relative error of at most 0.00043.
Values may be sent and summed in bfloat16 or wider, within the bound.
A program may use at most 128 MiB of HBM per device.

v0:
```python
import jax
import jax.numpy as jnp
from jax import lax
from jax.sharding import PartitionSpec as P


def pair_weights(kern_rows, share_rows, target_rows, row_count):
    pivot_ids = jnp.arange(row_count, dtype=jnp.int32)
    first_hit = (pivot_ids[None, :, None] == target_rows[:, None, :]).astype(jnp.float32)
    second_hit = (pivot_ids[None, :, None] == target_rows[:, None, :] + 1).astype(jnp.float32)
    weights = (
        0.5
        * kern_rows[:, None, :]
        * (share_rows[:, None, :] * first_hit + (1.0 - share_rows[:, None, :]) * second_hit)
    )
    return weights.astype(jnp.bfloat16)


def upstream_top(top_face, upstream, blk_id):
    gathered = lax.all_gather(top_face[None], "blk", axis=0, tiled=True)
    arrived = lax.dynamic_index_in_dim(gathered, upstream[blk_id], 0, keepdims=False)
    return arrived


def inflow_face(top_face, upstream, face_row, blk_id):
    return jnp.take(upstream_top(top_face, upstream, blk_id), face_row, axis=1)


def tendency(field_now, source, inflow, cour_rows):
    previous = jnp.concatenate([inflow[:, None, :], field_now[:, :-1, :]], axis=1)
    return -cour_rows[:, None, None] * (field_now - previous) + source


def source_terms(births, field_flat, full_flat, kern_rows, frag_rows, rate_rows):
    loss = jnp.dot(kern_rows, full_flat, preferred_element_type=jnp.float32)
    gain = jnp.dot(frag_rows, full_flat, preferred_element_type=jnp.float32)
    return births - field_flat * loss + gain - rate_rows[:, None] * field_flat


def shards(
    density,
    agg_kernel,
    pair_share,
    pair_target,
    fragments,
    break_rate,
    courant,
    block_rows,
    upstream,
    face_map,
):
    num_piv = agg_kernel.shape[0]
    own_piv, height, width = density.shape
    n_cells = height * width
    pair_id = lax.axis_index("pair")
    blk_id = lax.axis_index("blk")
    first_piv = pair_id * own_piv
    live_rows = block_rows[blk_id]
    live = (jnp.arange(height, dtype=jnp.int32) < live_rows)[None, :, None]
    face_row = face_map[0]
    pivot_ids = jnp.arange(num_piv, dtype=jnp.int32)
    smaller = (pivot_ids[:, None] < pivot_ids[None, :]).astype(jnp.float32)
    frag_b = (fragments * break_rate[None, :] * smaller).astype(jnp.bfloat16)
    kern_b = agg_kernel.astype(jnp.bfloat16)

    def rows_of(table):
        return lax.dynamic_slice_in_dim(table, first_piv, own_piv, 0)

    kern_mine = rows_of(agg_kernel)
    share_mine = rows_of(pair_share)
    target_mine = rows_of(pair_target)
    field_now = density
    for section_no in range(2):
        mine_b = field_now.astype(jnp.bfloat16)
        full_b = lax.all_gather(mine_b, "pair", axis=0, tiled=True)
        full_flat = full_b.reshape(num_piv, n_cells)
        mine_flat = mine_b.reshape(own_piv, n_cells)
        row_count = own_piv * lax.axis_size("pair")
        weights = pair_weights(kern_mine, share_mine, target_mine, row_count)
        inner = jnp.dot(
            weights.reshape(own_piv * row_count, num_piv),
            full_flat,
            preferred_element_type=jnp.float32,
        )
        inner = inner.reshape(own_piv, row_count, full_flat.shape[1])
        births = lax.psum_scatter(
            jnp.sum(mine_flat.astype(jnp.float32)[:, None, :] * inner, axis=0),
            "pair",
            scatter_dimension=0,
            tiled=True,
        )
        source = source_terms(
            births,
            field_now.reshape(own_piv, n_cells),
            full_flat,
            rows_of(kern_b),
            rows_of(frag_b),
            rows_of(break_rate),
        )
        inflow = inflow_face(
            lax.dynamic_index_in_dim(field_now, live_rows - 1, 1, keepdims=False),
            upstream,
            face_row,
            blk_id,
        )
        change = tendency(
            field_now, source.reshape(own_piv, height, width), inflow, rows_of(courant)
        )
        if section_no == 0:
            field_now = jnp.where(live, field_now + change, 0.0)
        else:
            field_now = jnp.where(live, 0.5 * density + 0.5 * (field_now + change), 0.0)
    return field_now


def solution(mesh):
    in_specs = (P("pair", "blk", None), P(), P(), P(), P(), P(), P(), P(), P(), P("blk", None))
    out_specs = P("pair", "blk", None)
    return jax.shard_map(shards, mesh=mesh, in_specs=in_specs, out_specs=out_specs, check_vma=False)
```

profile of v0, /device:TPU:1, one launch (start us, length us, event | category | flops | bytes accessed | tf_op | source)
XLA Modules:
  0.0 546.0 jit_solution(14339467940012295723)
XLA Ops:
  6.5 1.9 convert_element_type.63
  8.6 1.3 dynamic_slice.49
  11.1 1.0 pad.8
  12.2 1.4 copy.25
  13.6 0.7 dynamic_slice.46
  15.7 28.3 %all-gather = f32[320,1,256]{2,1,0:T(1,128)S(1)} all-gather(f32[20,1,256]{2,1,0:T(1,128)S(1)} %constant_dynamic-slice_fusion.5), channel_id=2, replica_groups=mesh['blk'=16,'pair'=8] {'blk'}, dimensions={0}, use_global_device_ids=true | all-gather | bytes 348160 | tf_op jit(solution)/shard_map/all_gather | solution.py:20
  44.0 0.8 reduce
  45.5 0.8 broadcast_add_fusion
  46.2 0.8 broadcast_subtract_fusion
  47.1 26.6 %all-gather.5.cloned.1.call-done = bf16[160,32,256]{2,1,0:T(8,128)(2,1)} async-done(((bf16[20,32,256]{2,1,0:T(8,128)(2,1)}), bf16[160,32,256]{2,1,0:T(8,128)(2,1)}) %all-gather.5.cloned.1.call-update) | async-done | bytes 2621456 | tf_op jit(solution)/shard_map/all_gather | solution.py:75
  73.7 3.9 reshape.159
  77.6 18.4 %multiply_reduce_fusion.1 = f32[160,8192]{1,0:T(8,128)} fusion(bf16[160,8192,1]{1,0,2:T(8,128)(2,1)S(1)} %reshape.159, f32[20,8192]{1,0:T(8,128)} %bitcast.72, f32[20,160]{1,0:T(8,128)S(1)} %get-tuple-element.10, s32[20,160]{1,0:T(8,128)S(1)} %get-tuple-element.8, f32[20,160]{1,0:T(8,128)S(1)} %get-tuple-element.11, s32[20,160]{1,0:T(8,128)S(1)} %get-tuple-element.9, ...), kind=kOutput, calls=%fused_computation.3 | convolution fusion | flops 8443310080 | bytes 8583680 | tf_op jit(solution)/shard_map/dot_general | solution.py:80
  96.0 128.7 %fusion = f32[24,8192]{1,0:T(8,128)} fusion(f32[160,8192]{1,0:T(8,128)} %multiply_reduce_fusion.1), kind=kCustom, calls=%all-reduce-scatter | all-reduce-scatter fusion | flops 1572865 | bytes 6029824
  224.7 2.3 collective-permute-start
  227.1 0.6 dynamic_slice.56
  227.7 1.4 copy.26
  229.2 0.7 gather_fusion
  230.1 0.6 dynamic-slice.6
  231.3 1.3 iota_compare_fusion.3
  232.6 0.7 dynamic-slice_negate_fusion
  233.3 1.0 slice.13
  234.2 7.6 %collective-permute-start.1 = (f32[4,8192]{1,0:T(4,128)S(1)}, f32[4,8192]{1,0:T(4,128)S(1)}, u32[]{:S(2)}, u32[]{:S(2)}) collective-permute-start(f32[4,8192]{1,0:T(4,128)S(1)} %slice.13), channel_id=1, source_target_pairs={{0,2},{1,3},{2,4},{3,5},{4,6},{5,7},{8,10},{9,11},{10,12},{11,13},... | collective-permute-start | bytes 393224
  241.8 3.5 copy.27
  245.4 2.1 fusion.23
  247.5 11.5 %concatenate.8 = f32[52,8192]{1,0:T(8,128)} concatenate(f32[4,8192]{1,0:T(4,128)S(1)} %collective-permute-done.1, f32[24,8192]{1,0:T(8,128)} %collective-permute-done, f32[24,8192]{1,0:T(8,128)} %fusion), dimensions={0} | concatenate | bytes 3407872
  259.0 2.2 fusion.8
  261.3 0.3 copy.28
  261.6 1.1 fusion.27
  262.7 1.3 pad.10
  263.9 0.5 copy.29
  264.5 1.4 copy.30
  265.9 60.2 %all-gather.7.cloned.1.call-done = bf16[160,32,256]{2,1,0:T(8,128)(2,1)} async-done(((bf16[20,32,256]{2,1,0:T(8,128)(2,1)}), bf16[160,32,256]{2,1,0:T(8,128)(2,1)}) %all-gather.7.cloned.1.call-update) | async-done | bytes 2621456 | tf_op jit(solution)/shard_map/all_gather | solution.py:75
  326.1 5.3 reshape.160
  331.3 19.0 %multiply_reduce_fusion = f32[160,8192]{1,0:T(8,128)} fusion(bf16[160,8192,1]{1,0,2:T(8,128)(2,1)} %reshape.160, f32[20,8192]{1,0:T(8,128)S(1)} %bitcast.73, f32[20,160]{1,0:T(8,128)S(1)} %get-tuple-element.10, s32[20,160]{1,0:T(8,128)S(1)} %get-tuple-element.8, f32[20,160]{1,0:T(8,128)S(1)} %get-tuple-element.11, s32[20,160]{1,0:T(8,128)S(1)} %get-tuple-element.9, ...), kind=kOutput, calls=%fused_computation.2 | convolution fusion | flops 8443310080 | bytes 8583680 | tf_op jit(solution)/shard_map/dot_general | solution.py:80
  350.3 133.0 %fusion.1 = f32[24,8192]{1,0:T(8,128)} fusion(f32[160,8192]{1,0:T(8,128)} %multiply_reduce_fusion), kind=kCustom, calls=%all-reduce-scatter.1 | all-reduce-scatter fusion | flops 1572865 | bytes 6029824
  483.3 2.2 collective-permute-start.2
  485.5 22.2 %all-gather.1 = f32[320,1,256]{2,1,0:T(1,128)S(1)} all-gather(f32[20,1,256]{2,1,0:T(1,128)S(1)} %constant_dynamic-slice_fusion.1), channel_id=3, replica_groups=mesh['blk'=16,'pair'=8] {'blk'}, dimensions={0}, use_global_device_ids=true | all-gather | bytes 348160 | tf_op jit(solution)/shard_map/all_gather | solution.py:20
  507.7 0.8 reduce.1
  508.6 0.1 copy.21
  508.7 0.7 gather_fusion.1
  509.6 1.0 slice.14
  510.6 7.5 %collective-permute-start.3 = (f32[4,8192]{1,0:T(4,128)S(1)}, f32[4,8192]{1,0:T(4,128)S(1)}, u32[]{:S(2)}, u32[]{:S(2)}) collective-permute-start(f32[4,8192]{1,0:T(4,128)S(1)} %slice.14), channel_id=1, source_target_pairs={{0,2},{1,3},{2,4},{3,5},{4,6},{5,7},{8,10},{9,11},{10,12},{11,13},... | collective-permute-start | bytes 393224
  518.1 3.5 copy.31
  521.7 2.2 fusion.25
  523.9 11.5 %concatenate.9 = f32[52,8192]{1,0:T(8,128)} concatenate(f32[4,8192]{1,0:T(4,128)S(1)} %collective-permute-done.3, f32[24,8192]{1,0:T(8,128)} %collective-permute-done.2, f32[24,8192]{1,0:T(8,128)} %fusion.1), dimensions={0} | concatenate | bytes 3407872
  535.4 2.3 fusion.6
  537.7 0.3 copy.32
  538.0 1.2 fusion.12
  (56 shorter events, 0.9 us)
Async XLA Ops:
  6.5 9.2 %copy-start = (f32[20,32,256]{2,1,0:T(8,128)S(1)}, f32[20,32,256]{2,1,0:T(8,128)}, u32[]{:S(2)}) copy-start(f32[20,32,256]{2,1,0:T(8,128)} %param.12) | copy-start | bytes 1966084
  6.5 7.1 %copy-start.15 = (s32[16]{0:T(128)S(1)}, s32[16]{0:T(128)}, u32[]{:S(2)}) copy-start(s32[16]{0:T(128)} %param.19) | copy-start | bytes 196
  6.5 40.5 %copy-start.12 = (s32[1,256]{1,0:T(1,128)S(1)}, s32[1,256]{1,0:T(1,128)}, u32[]{:S(2)}) copy-start(s32[1,256]{1,0:T(1,128)} %param.21) | copy-start | bytes 3076
  6.5 67.1 %all-gather.5.cloned.1.call-start = ((), (), s32[]{:S(2)}) async-start(), calls=%async_computation | async-start | bytes 2949120 | tf_op jit(solution)/shard_map/all_gather | solution.py:75
  8.5 317.6 %all-gather.7.cloned.1.call-start = ((), (), s32[]{:S(2)}) async-start(), calls=%async_computation.1 | async-start | bytes 2949120 | tf_op jit(solution)/shard_map/all_gather | solution.py:75
  47.0 182.8 %copy-start.6 = (pred[256]{0:T(512)(128)(4,1)}, pred[256]{0:T(512)(128)(4,1)S(1)}, u32[]{:S(2)}) copy-start(pred[256]{0:T(512)(128)(4,1)S(1)} %compare_and_fusion) | copy-start | bytes 772
  96.0 131.1 %copy-start.3 = (f32[160]{0:T(256)S(1)}, f32[160]{0:T(256)}, u32[]{:S(2)}) copy-start(f32[160]{0:T(256)} %param.17) | copy-start | bytes 1924
  224.7 5.4 copy-start.13
  224.7 7.9 %copy-start.14 = (f32[160]{0:T(256)S(1)}, f32[160]{0:T(256)}, u32[]{:S(2)}) copy-start(f32[160]{0:T(256)} %param.18) | copy-start | bytes 1924
  224.7 22.9 %collective-permute-start = (f32[24,8192]{1,0:T(8,128)}, f32[24,8192]{1,0:T(8,128)}, u32[]{:S(2)}, u32[]{:S(2)}) collective-permute-start(f32[24,8192]{1,0:T(8,128)} %fusion), channel_id=1, source_target_pairs={{0,1},{1,2},{2,3},{3,4},{4,5},{5,6},{6,7},{8,9},{9,10},{10,11},{11... | collective-permute-start | bytes 2359304
  234.2 13.3 %collective-permute-start.1 = (f32[4,8192]{1,0:T(4,128)S(1)}, f32[4,8192]{1,0:T(4,128)S(1)}, u32[]{:S(2)}, u32[]{:S(2)}) collective-permute-start(f32[4,8192]{1,0:T(4,128)S(1)} %slice.13), channel_id=1, source_target_pairs={{0,2},{1,3},{2,4},{3,5},{4,6},{5,7},{8,10},{9,11},{10,12},{11,13},... | collective-permute-start | bytes 393224
  259.0 2.5 copy-start.8
  259.0 2.5 copy-start.10
  262.6 68.7 %copy-start.1 = (f32[20,32,256]{2,1,0:T(8,128)}, f32[20,32,256]{2,1,0:T(8,128)S(1)}, u32[]{:S(2)}) copy-start(f32[20,32,256]{2,1,0:T(8,128)S(1)} %get-tuple-element.7) | copy-start | bytes 1966084
  350.3 159.1 %copy-start.7 = (pred[256]{0:T(512)(128)(4,1)S(1)}, pred[256]{0:T(512)(128)(4,1)}, u32[]{:S(2)}) copy-start(pred[256]{0:T(512)(128)(4,1)} %copy-done.6) | copy-start | bytes 772
  483.3 40.5 %collective-permute-start.2 = (f32[24,8192]{1,0:T(8,128)}, f32[24,8192]{1,0:T(8,128)}, u32[]{:S(2)}, u32[]{:S(2)}) collective-permute-start(f32[24,8192]{1,0:T(8,128)} %fusion.1), channel_id=1, source_target_pairs={{0,1},{1,2},{2,3},{3,4},{4,5},{5,6},{6,7},{8,9},{9,10},{10,11},{11... | collective-permute-start | bytes 2359304
  508.5 13.1 %copy-start.4 = (f32[160]{0:T(256)S(1)}, f32[160]{0:T(256)}, u32[]{:S(2)}) copy-start(f32[160]{0:T(256)} %param.17) | copy-start | bytes 1924
  510.6 13.3 %collective-permute-start.3 = (f32[4,8192]{1,0:T(4,128)S(1)}, f32[4,8192]{1,0:T(4,128)S(1)}, u32[]{:S(2)}, u32[]{:S(2)}) collective-permute-start(f32[4,8192]{1,0:T(4,128)S(1)} %slice.14), channel_id=1, source_target_pairs={{0,2},{1,3},{2,4},{3,5},{4,6},{5,7},{8,10},{9,11},{10,12},{11,13},... | collective-permute-start | bytes 393224
  521.6 13.7 %copy-start.5 = (f32[20]{0:T(128)S(1)}, f32[20]{0:T(128)}, u32[]{:S(2)}) copy-start(f32[20]{0:T(128)} %dynamic_slice.56) | copy-start | bytes 244
  535.4 2.6 copy-start.2
  535.4 2.6 copy-start.9
  535.4 2.6 copy-start.11
Sparse Core Ops, SparseCore 0:
  9.0 64.6 all-gather.4
  262.8 63.2 all-gather.6
where the time goes:
time: 548 us; the launch traced here: 546 us
  blocking collectives  312 us (57%)
  waiting for transfers between devices  86.8 us (16%)
  local copies, waits for them, and re-layouts  54 us (10%)
  matrix products  46.3 us (8%)
  starting transfers between devices  19.6 us (4%)
  between operations  17.7 us (3%)
  other arithmetic  9.4 us (2%)
    unnamed x2, blocking collectives  262 us
    all_gather x2, waiting for transfers between devices, shards(): full_b = lax.all_gather(mine_b, 'pair', axis=0, tiled=True)  86.8 us
    all_gather x2, blocking collectives, upstream_top(): gathered = lax.all_gather(top_face[None], 'blk', axis=0, tiled=True)  50.5 us
    unnamed x49, local copies, waits for them, and re-layouts  40.4 us
    dot_general x2, matrix products, shards(): jnp.dot(weights.reshape(own_piv * row_count, num_piv), full_flat, preferr...  37.4 us
    unnamed x4, starting transfers between devices  19.5 us
  transfers between devices with their start and end apart: 6, of which 2 were waited for; matrix products, arithmetic and copies ran while one was open for 6% of the time, Pallas kernels for 0%

commit v1 on v0

v1 whole, which is shorter than its diff:
```python
import functools

import jax
import jax.numpy as jnp
from jax import lax
from jax.experimental import pallas as pl
from jax.experimental.pallas import tpu as pltpu
from jax.sharding import PartitionSpec as P

MESH = pl.DeviceIdType.MESH
BANDS = 5
F32 = jnp.float32
BF16 = jnp.bfloat16


def permuted(face, one_hot):
    total = None
    for _ in range(3):
        part = face.astype(BF16)
        face = face - part.astype(F32)
        moved = jnp.dot(part, one_hot, preferred_element_type=F32)
        total = moved if total is None else total + moved
    return total


def step_kernel(
    n_blk, n_pair, own, piv, height, width,
    density, agg, share, target, frag, rate, cour, rows_sm, up_sm, face_map,
    main, add,
    dens_v, v0, sec, out, wb, y_s, faces, faces2, halo_s, halo_r, halo_c, edge_r, top_s, top_p, top_r,
    local_sem, main_send, main_recv, face_send, face_recv, face2_send, face2_recv,
    halo_send, halo_recv, edge_send, edge_recv, top_send, top_recv, out_send, out_recv,
):
    me_b, me_p = lax.axis_index("blk"), lax.axis_index("pair")
    grp, half = me_p // 2, me_p % 2
    pairs = [lax.rem(me_p + d, n_pair) for d in range(n_pair)]
    blks = [lax.rem(me_b + d, n_blk) for d in range(n_blk)]

    def tile_of(ref, p):
        return ref.at[:, pl.ds(pl.multiple_of((p // 2) * 8, 8), 8), pl.ds(pl.multiple_of((p % 2) * 128, 128), 128)]

    loads = [pltpu.make_async_copy(density.at[:, :, pl.ds(t * 128, 128)], dens_v.at[t], local_sem.at[5 + t])
             for t in range(2)]
    for load in loads:
        load.start()
    load_own = pltpu.make_async_copy(tile_of(density, me_p), v0.at[pl.ds(me_p * own, own)], local_sem.at[1])
    load_own.start()

    barrier = pltpu.get_barrier_semaphore()
    for d in range(1, n_pair):
        pl.semaphore_signal(barrier, inc=1, device_id=(me_b, pairs[d]), device_id_type=MESH)
    for d in range(1, n_blk):
        pl.semaphore_signal(barrier, inc=1, device_id=(blks[d], me_p), device_id_type=MESH)
    pl.semaphore_wait(barrier, n_pair + n_blk - 2)

    def to_pair(d, src, dst, send, recv):
        return pltpu.make_async_remote_copy(
            src_ref=src, dst_ref=dst, send_sem=send.at[d], recv_sem=recv.at[d],
            device_id=(me_b, pairs[d]), device_id_type=MESH)

    def to_blk(d, src, dst, send, recv):
        return pltpu.make_async_remote_copy(
            src_ref=src, dst_ref=dst, send_sem=send.at[d], recv_sem=recv.at[d],
            device_id=(blks[d], me_p), device_id_type=MESH)

    main_in = [to_pair(d, tile_of(density, pairs[d]), v0.at[pl.ds(me_p * own, own)], main_send, main_recv)
               for d in range(1, n_pair)]
    for copy in main_in:
        copy.start()

    for load in loads:
        load.wait()
    dens_rows = dens_v.reshape(2 * own * height, 128)
    for t in range(2):
        faces[me_b, :, pl.ds(t * 128, 128)] = dens_rows[
            pl.ds(jnp.maximum(rows_sm[me_b] - 1, 0) + t * own * height, own, stride=height), :]
    faces_out = [to_blk(d, faces.at[me_b], faces.at[me_b], face_send, face_recv) for d in range(1, n_blk)]
    for copy in faces_out:
        copy.start()
    for q in range(1, height // 8):
        for t in range(2):
            halo_s[q, :, pl.ds(t * 128, 128)] = dens_rows[
                pl.ds(8 * q - 1 + t * own * height, own, stride=height), :]

    row_id = lax.broadcasted_iota(jnp.int32, (piv, piv), 0)
    col_id = lax.broadcasted_iota(jnp.int32, (piv, piv), 1)
    kern = agg[...]
    part = share[...]
    low = (0.5 * kern * part).astype(BF16).astype(F32)
    high = (0.5 * kern * (1.0 - part)).astype(BF16).astype(F32)
    offset = (target[...] - jnp.maximum(row_id, col_id)).astype(F32)
    last = []
    for n, (lo, hi, off, keep) in enumerate((
        (low, high, offset, col_id <= row_id),
        (low.T, high.T, offset.T, col_id < row_id),
    )):
        for d in range(BANDS):
            band = jnp.where(off == d, lo, jnp.where(off == d - 1, hi, 0.0))
            wb[pl.ds((n * BANDS + d) * piv, piv), :] = jnp.where(keep, band, 0.0).astype(BF16)
        last.append(pltpu.roll(jnp.where(keep & (off == -1), lo, 0.0)[piv - 8:], 7, 0))
    rate_row = rate[...]
    base = 2 * BANDS * piv
    wb[pl.ds(base, piv), :] = kern.astype(BF16)
    wb[pl.ds(base + 2 * piv, 16), :] = jnp.concatenate(last, axis=0).astype(BF16)
    smaller = (row_id < col_id).astype(F32)
    wb[pl.ds(base + piv, piv), :] = (frag[...] * rate_row * smaller).astype(BF16)
    diag = row_id == col_id
    rate_col = jnp.sum(jnp.where(diag, rate_row, 0.0), axis=1, keepdims=True)
    cour_col = jnp.sum(jnp.where(diag, cour[...], 0.0), axis=1, keepdims=True)

    one_hot = (lax.broadcasted_iota(jnp.int32, (width, width), 0) == face_map[...]).astype(F32).astype(BF16)

    for copy in faces_out:
        copy.wait_recv()
    halo_s[0] = permuted(faces[up_sm[me_b]], one_hot)

    def halo_of(p):
        return halo_s.at[p // 2, :, pl.ds(pl.multiple_of((p % 2) * 128, 128), 128)]

    halos = [to_pair(d, halo_of(pairs[d]), halo_r.at[me_p], halo_send, halo_recv) for d in range(1, n_pair)]
    for copy in halos:
        copy.start()
    halo_own = pltpu.make_async_copy(halo_of(me_p), halo_r.at[me_p], local_sem.at[2])
    halo_own.start()

    live_rows = rows_sm[me_b]
    top_row = live_rows - 1

    def change(v, prev):
        y_s[...] = jnp.dot(wb[...], v.astype(BF16), preferred_element_type=F32)
        vb = v.astype(BF16).astype(F32)
        below = y_s[pl.ds(base + 2 * piv, 8), :] + y_s[pl.ds(base + 2 * piv + 8, 8), :]
        y_s[pl.ds(base + 2 * piv - 8, 8), :] += below * vb[piv - 1:]
        births = None
        for d in reversed(range(BANDS)):
            here = vb * (y_s[pl.ds(d * piv, piv), :] + y_s[pl.ds((BANDS + d) * piv, piv), :])
            births = here if births is None else here + pltpu.roll(births, 1, 0)
        loss = y_s[pl.ds(base, piv), :]
        gain = y_s[pl.ds(base + piv, piv), :]
        source = births - v * loss + gain - rate_col * v
        return v + (source - cour_col * (v - prev))

    v0_rows = v0.reshape(piv * 8, 128)
    out_rows = out.reshape(piv * 8, 128)

    def start_row(s):
        return v0_rows[pl.ds(s, piv, stride=8), :]

    load_own.wait()
    for copy in main_in:
        copy.wait_recv()

    top = None
    edge = to_pair(
        2, sec.at[:, pl.ds(7 * 128, 128)], edge_r, edge_send, edge_recv)
    for it in reversed(range(4)):
        s = 2 * it
        if it == 0:
            halo_own.wait()
            for copy in halos:
                copy.wait_recv()
            for p in range(n_pair):
                halo_c[pl.ds(p * own, own), :] = halo_r[p]
            before = halo_c[...]
        else:
            before = start_row(s - 1)
        first, second = start_row(s), start_row(s + 1)
        now = change(jnp.concatenate([first, second], axis=1), jnp.concatenate([before, first], axis=1))
        for t in range(2):
            row = grp * 8 + s + t
            piece = jnp.where(row < live_rows, now[:, t * 128:(t + 1) * 128], 0.0)
            sec[:, pl.ds((s + t) * 128, 128)] = piece
            mine = jnp.where(row == top_row, piece, 0.0)
            top = mine if top is None else top + mine
        if it == 3:
            edge.start()

    top_s[...] = 0.5 * cour_col * top
    for p in range(n_pair):
        top_p[p] = top_s[pl.ds(p * own, own), :]
    tops = [to_pair(d, top_p.at[pairs[d]], top_r.at[me_p], top_send, top_recv) for d in range(1, n_pair)]
    for copy in tops:
        copy.start()
    top_own = pltpu.make_async_copy(top_p.at[me_p], top_r.at[me_p], local_sem.at[3])
    top_own.start()

    for it in reversed(range(4)):
        s = 2 * it
        if it == 0:
            top_own.wait()
            for copy in tops:
                copy.wait_recv()
            for t in range(2):
                faces2[me_b, :, pl.ds(t * 128, 128)] = (top_r[t] + top_r[t + 2]) + (top_r[t + 4] + top_r[t + 6])
            faces2_out = [to_blk(d, faces2.at[me_b], faces2.at[me_b], face2_send, face2_recv)
                          for d in range(1, n_blk)]
            for copy in faces2_out:
                copy.start()
            edge.wait_recv()
            before = jnp.where(grp > 0, edge_r[...], 0.0)
        else:
            before = sec[:, pl.ds((s - 1) * 128, 128)]
        v = sec[:, pl.ds(s * 128, 256)]
        now = change(v, jnp.concatenate([before, v[:, :128]], axis=1))
        for t in range(2):
            row = grp * 8 + s + t
            piece = 0.5 * start_row(s + t) + 0.5 * now[:, t * 128:(t + 1) * 128]
            out_rows[pl.ds(s + t, piv, stride=8), :] = jnp.where(row < live_rows, piece, 0.0)

    outs = [to_pair(d, out.at[pl.ds(pairs[d] * own, own)], tile_of(main, me_p), out_send, out_recv)
            for d in range(1, n_pair)]
    for copy in outs:
        copy.start()
    out_own = pltpu.make_async_copy(out.at[pl.ds(me_p * own, own)], tile_of(main, me_p), local_sem.at[4])
    out_own.start()

    for copy in faces2_out:
        copy.wait_recv()
    add[...] = permuted(faces2[up_sm[me_b]], one_hot)

    out_own.wait()
    for copy in outs:
        copy.wait_recv()
    for copy in main_in + faces_out + halos + [edge] + tops + faces2_out + outs:
        copy.wait_send()


def shards(n_blk, n_pair, density, agg, share, target, frag, rate, cour, block_rows, upstream, face_map):
    own, height, width = density.shape
    piv = agg.shape[0]
    vmem = pl.BlockSpec(memory_space=pltpu.VMEM)
    smem = pl.BlockSpec(memory_space=pltpu.SMEM)
    hbm = pl.BlockSpec(memory_space=pl.ANY)
    dma = pltpu.SemaphoreType.DMA
    main, add = pl.pallas_call(
        functools.partial(step_kernel, n_blk, n_pair, own, piv, height, width),
        out_shape=(
            jax.ShapeDtypeStruct(density.shape, F32),
            jax.ShapeDtypeStruct((own, width), F32),
        ),
        in_specs=[hbm] + [vmem] * 6 + [smem] * 2 + [vmem],
        out_specs=(hbm, vmem),
        scratch_shapes=[
            pltpu.VMEM((2, own, height, 128), F32),
            pltpu.VMEM((piv, 8, 128), F32),
            pltpu.VMEM((piv, 1024), F32),
            pltpu.VMEM((piv, 8, 128), F32),
            pltpu.VMEM(((2 * BANDS + 2) * piv + 16, piv), BF16),
            pltpu.VMEM(((2 * BANDS + 2) * piv + 16, 256), F32),
            pltpu.VMEM((n_blk, own, width), F32),
            pltpu.VMEM((n_blk, own, width), F32),
            pltpu.VMEM((height // 8, own, width), F32),
            pltpu.VMEM((n_pair, own, 128), F32),
            pltpu.VMEM((piv, 128), F32),
            pltpu.VMEM((piv, 128), F32),
            pltpu.VMEM((piv, 128), F32),
            pltpu.VMEM((n_pair, own, 128), F32),
            pltpu.VMEM((n_pair, own, 128), F32),
            dma((7,)),
            dma((n_pair,)), dma((n_pair,)),
            dma((n_blk,)), dma((n_blk,)),
            dma((n_blk,)), dma((n_blk,)),
            dma((n_pair,)), dma((n_pair,)),
            dma((n_pair,)), dma((n_pair,)),
            dma((n_pair,)), dma((n_pair,)),
            dma((n_pair,)), dma((n_pair,)),
        ],
        compiler_params=pltpu.CompilerParams(
            collective_id=0, has_side_effects=True, vmem_limit_bytes=40 * 1024 * 1024),
    )(density, agg, share, target, frag, rate.reshape(1, piv), cour.reshape(1, piv), block_rows, upstream, face_map)
    bottom = lax.broadcasted_iota(jnp.int32, main.shape, 1) == 0
    return jnp.where(bottom, main + add[:, None, :], main)


def solution(mesh):
    in_specs = (P("pair", "blk", None), P(), P(), P(), P(), P(), P(), P(), P(), P("blk", None))
    out_specs = P("pair", "blk", None)
    return jax.shard_map(
        functools.partial(shards, mesh.shape["blk"], mesh.shape["pair"]),
        mesh=mesh, in_specs=in_specs, out_specs=out_specs, check_vma=False)
```

time: 548 us -> 51.8 us (0.09)
  blocking collectives: 312 us -> 0 us
  waiting for transfers between devices: 86.8 us -> 0 us
  local copies, waits for them, and re-layouts: 54 us -> 5.44 us
  matrix products: 46.3 us -> 0 us
  Pallas kernels: 0 us -> 45 us
  starting transfers between devices: 19.6 us -> 0 us
  between operations: 17.7 us -> 0.04 us
  other arithmetic: 9.4 us -> 1.01 us
    unnamed x2 -> x0, blocking collectives: 262 us -> none
    all_gather x2 -> x0, waiting for transfers between devices: 86.8 us -> none  [shards(): full_b = lax.all_gather(mine_b, 'pair', axis=0, tiled=True)]
    all_gather x2 -> x0, blocking collectives: 50.5 us -> none  [upstream_top(): gathered = lax.all_gather(top_face[None], 'blk', axis=0, tiled=True)]
    dot_general x6 -> x0, matrix products: 46.3 us -> none  [the longest x2 37.4 us: shards(): jnp.dot(weights.reshape(own_piv * row_count, num_piv), full_flat, preferr...]
    pallas_call x0 -> x1, Pallas kernels: none -> 45 us  [shards(): pl.pallas_call(functools.partial(step_kernel, n_blk, n_pair, own, piv, he...]
    unnamed x49 -> x20, local copies, waits for them, and re-layouts: 40.4 us -> 5.44 us
    unnamed x4 -> x0, starting transfers between devices: 19.5 us -> none
    reshape x2 -> x0, local copies, waits for them, and re-layouts: 9.13 us -> none  [shards(): full_flat = full_b.reshape(num_piv, n_cells)]
  transfers between devices with their start and end apart: 6 -> 0, of which waited for: 2 -> 0; matrix products, arithmetic and copies ran while one was open for 6% -> 0% of each run, Pallas kernels for 0% -> 0%
where the time goes in v1:
time: 51.8 us; the launch traced here: 51.5 us
  Pallas kernels  45 us (87%)
  local copies, waits for them, and re-layouts  5.44 us (11%)
  other arithmetic  1.01 us (2%)
    pallas_call x1, Pallas kernels, shards(): pl.pallas_call(functools.partial(step_kernel, n_blk, n_pair, own, piv, he...  45 us
    unnamed x20, local copies, waits for them, and re-layouts  5.44 us

profile of v1, /device:TPU:1, one launch (start us, length us, event | category | flops | bytes accessed | tf_op | source)
XLA Modules:
  0.0 51.5 jit_solution(10463361400473465506)
XLA Ops:
  0.0 0.0 copy-start.9
  0.0 0.0 copy-start.6
  0.0 0.0 copy-start.7
  0.0 0.0 copy-start.5
  0.0 0.0 copy-start.8
  0.0 0.6 %copy-done.9 = s32[16]{0:T(128)S(1)} copy-done((s32[16]{0:T(128)S(1)}, s32[16]{0:T(128)}, u32[]{:S(2)}) %copy-start.9) | copy-done | bytes 88
  0.7 0.0 copy-done.6
  0.7 0.0 copy-done.7
  0.7 0.0 copy-done.5
  0.7 0.0 copy-done.8
  0.7 0.0 copy-start
  0.7 1.1 %copy-done = f32[20,32,256]{2,1,0:T(8,128)S(1)} copy-done((f32[20,32,256]{2,1,0:T(8,128)S(1)}, f32[20,32,256]{2,1,0:T(8,128)}, u32[]{:S(2)}) %copy-start) | copy-done | bytes 655384
  1.8 0.0 copy-start.1
  1.8 0.9 %copy-done.1 = f32[160,160]{1,0:T(8,128)S(1)} copy-done((f32[160,160]{1,0:T(8,128)S(1)}, f32[160,160]{1,0:T(8,128)}, u32[]{:S(2)}) %copy-start.1) | copy-done | bytes 102424
  2.7 0.0 copy-start.2
  2.7 0.9 %copy-done.2 = f32[160,160]{1,0:T(8,128)S(1)} copy-done((f32[160,160]{1,0:T(8,128)S(1)}, f32[160,160]{1,0:T(8,128)}, u32[]{:S(2)}) %copy-start.2) | copy-done | bytes 102424
  3.7 0.0 copy-start.3
  3.7 0.9 %copy-done.3 = s32[160,160]{1,0:T(8,128)S(1)} copy-done((s32[160,160]{1,0:T(8,128)S(1)}, s32[160,160]{1,0:T(8,128)}, u32[]{:S(2)}) %copy-start.3) | copy-done | bytes 102424
  4.6 0.0 copy-start.4
  4.6 0.9 %copy-done.4 = f32[160,160]{1,0:T(8,128)S(1)} copy-done((f32[160,160]{1,0:T(8,128)S(1)}, f32[160,160]{1,0:T(8,128)}, u32[]{:S(2)}) %copy-start.4) | copy-done | bytes 102424
  5.5 45.0 %shard_map.100 = (f32[20,32,256]{2,1,0:T(8,128)S(1)}, f32[20,256]{1,0:T(8,128)S(1)}) custom-call(f32[20,32,256]{2,1,0:T(8,128)S(1)} %copy-done, f32[160,160]{1,0:T(8,128)S(1)} %copy-done.1, f32[160,160]{1,0:T(8,128)S(1)} %copy-done.2, s32[160,160]{1,0:T(8,128)S(1)} %copy-done.3, f32[160,160]{1,0:T(8,128)S(1)} %copy-done.4, f32[1,160]{1,0:T(1,128)S(1)} %bitcast.2, ...), custom_call_target="tpu_custom_call" | custom-call | tf_op jit(solution)/shard_map/pallas_call | solution.py:235
  50.5 1.0 %add_select_fusion = f32[20,32,256]{2,1,0:T(8,128)} fusion(f32[20,32,256]{2,1,0:T(8,128)S(1)} %get-tuple-element.7, f32[20,256]{1,0:T(8,128)S(1)} %get-tuple-element.8, pred[32]{0:T(512)(128)(4,1)S(1)} %iota_compare_fusion), kind=kLoop, calls=%fused_computation | loop fusion | flops 327680 | bytes 1331232 | tf_op jit(solution)/shard_map/jit(_where)/select_n | solution.py:272
  (1 shorter events, 0.0 us)
Async XLA Ops:
  0.0 0.7 %copy-start.9 = (s32[16]{0:T(128)S(1)}, s32[16]{0:T(128)}, u32[]{:S(2)}) copy-start(s32[16]{0:T(128)} %up_sm.1) | copy-start | bytes 196
  0.0 0.7 %copy-start.6 = (f32[160]{0:T(256)S(1)}, f32[160]{0:T(256)}, u32[]{:S(2)}) copy-start(f32[160]{0:T(256)} %param.16) | copy-start | bytes 1924
  0.0 0.7 %copy-start.7 = (s32[1,256]{1,0:T(1,128)S(1)}, s32[1,256]{1,0:T(1,128)}, u32[]{:S(2)}) copy-start(s32[1,256]{1,0:T(1,128)} %face_map.1) | copy-start | bytes 3076
  0.0 0.7 %copy-start.5 = (f32[160]{0:T(256)S(1)}, f32[160]{0:T(256)}, u32[]{:S(2)}) copy-start(f32[160]{0:T(256)} %param.15) | copy-start | bytes 1924
  0.0 0.7 %copy-start.8 = (s32[16]{0:T(128)S(1)}, s32[16]{0:T(128)}, u32[]{:S(2)}) copy-start(s32[16]{0:T(128)} %rows_sm.1) | copy-start | bytes 196
  0.7 1.1 %copy-start = (f32[20,32,256]{2,1,0:T(8,128)S(1)}, f32[20,32,256]{2,1,0:T(8,128)}, u32[]{:S(2)}) copy-start(f32[20,32,256]{2,1,0:T(8,128)} %density.1) | copy-start | bytes 1966084
  1.8 0.9 %copy-start.1 = (f32[160,160]{1,0:T(8,128)S(1)}, f32[160,160]{1,0:T(8,128)}, u32[]{:S(2)}) copy-start(f32[160,160]{1,0:T(8,128)} %agg.1) | copy-start | bytes 307204
  2.7 0.9 %copy-start.2 = (f32[160,160]{1,0:T(8,128)S(1)}, f32[160,160]{1,0:T(8,128)}, u32[]{:S(2)}) copy-start(f32[160,160]{1,0:T(8,128)} %share.1) | copy-start | bytes 307204
  3.7 0.9 %copy-start.3 = (s32[160,160]{1,0:T(8,128)S(1)}, s32[160,160]{1,0:T(8,128)}, u32[]{:S(2)}) copy-start(s32[160,160]{1,0:T(8,128)} %target.1) | copy-start | bytes 307204
  4.6 0.9 %copy-start.4 = (f32[160,160]{1,0:T(8,128)S(1)}, f32[160,160]{1,0:T(8,128)}, u32[]{:S(2)}) copy-start(f32[160,160]{1,0:T(8,128)} %frag.1) | copy-start | bytes 307204

commit v2 on v1

--- a/solution.py
+++ b/solution.py
@@ -25,9 +25,9 @@
 
 def step_kernel(
     n_blk, n_pair, own, piv, height, width,
-    density, agg, share, target, frag, rate, cour, rows_sm, up_sm, face_map,
+    density, agg_h, share_h, target_h, frag_h, rate, cour, rows_sm, up_sm, face_map,
     main, add,
-    dens_v, v0, sec, out, wb, y_s, faces, faces2, halo_s, halo_r, halo_c, edge_r, top_s, top_p, top_r,
+    agg, share, target, frag, dens_v, v0, sec, out, wb, y_s, faces, faces2, halo_s, halo_r, halo_c, edge_r, top_s, top_p, top_r,
     local_sem, main_send, main_recv, face_send, face_recv, face2_send, face2_recv,
     halo_send, halo_recv, edge_send, edge_recv, top_send, top_recv, out_send, out_recv,
 ):
@@ -45,6 +45,10 @@
         load.start()
     load_own = pltpu.make_async_copy(tile_of(density, me_p), v0.at[pl.ds(me_p * own, own)], local_sem.at[1])
     load_own.start()
+    tables = [pltpu.make_async_copy(src, dst, local_sem.at[7 + n]) for n, (src, dst) in enumerate(
+        ((agg_h, agg), (share_h, share), (target_h, target), (frag_h, frag)))]
+    for load in tables:
+        load.start()
 
     barrier = pltpu.get_barrier_semaphore()
     for d in range(1, n_pair):
@@ -82,6 +86,8 @@
             halo_s[q, :, pl.ds(t * 128, 128)] = dens_rows[
                 pl.ds(8 * q - 1 + t * own * height, own, stride=height), :]
 
+    for load in tables:
+        load.wait()
     row_id = lax.broadcasted_iota(jnp.int32, (piv, piv), 0)
     col_id = lax.broadcasted_iota(jnp.int32, (piv, piv), 1)
     kern = agg[...]
@@ -230,7 +236,7 @@
     piv = agg.shape[0]
     vmem = pl.BlockSpec(memory_space=pltpu.VMEM)
     smem = pl.BlockSpec(memory_space=pltpu.SMEM)
-    hbm = pl.BlockSpec(memory_space=pl.ANY)
+    hbm = pl.BlockSpec(memory_space=pltpu.HBM)
     dma = pltpu.SemaphoreType.DMA
     main, add = pl.pallas_call(
         functools.partial(step_kernel, n_blk, n_pair, own, piv, height, width),
@@ -238,9 +244,13 @@
             jax.ShapeDtypeStruct(density.shape, F32),
             jax.ShapeDtypeStruct((own, width), F32),
         ),
-        in_specs=[hbm] + [vmem] * 6 + [smem] * 2 + [vmem],
+        in_specs=[hbm] * 5 + [vmem] * 2 + [smem] * 2 + [vmem],
         out_specs=(hbm, vmem),
         scratch_shapes=[
+            pltpu.VMEM((piv, piv), F32),
+            pltpu.VMEM((piv, piv), F32),
+            pltpu.VMEM((piv, piv), jnp.int32),
+            pltpu.VMEM((piv, piv), F32),
             pltpu.VMEM((2, own, height, 128), F32),
             pltpu.VMEM((piv, 8, 128), F32),
             pltpu.VMEM((piv, 1024), F32),
@@ -256,7 +266,7 @@
             pltpu.VMEM((piv, 128), F32),
             pltpu.VMEM((n_pair, own, 128), F32),
             pltpu.VMEM((n_pair, own, 128), F32),
-            dma((7,)),
+            dma((11,)),
             dma((n_pair,)), dma((n_pair,)),
             dma((n_blk,)), dma((n_blk,)),
             dma((n_blk,)), dma((n_blk,)),
@@ -266,7 +276,7 @@
             dma((n_pair,)), dma((n_pair,)),
         ],
         compiler_params=pltpu.CompilerParams(
-            collective_id=0, has_side_effects=True, vmem_limit_bytes=40 * 1024 * 1024),
+            collective_id=0, has_side_effects=True, vmem_limit_bytes=56 * 1024 * 1024),
     )(density, agg, share, target, frag, rate.reshape(1, piv), cour.reshape(1, piv), block_rows, upstream, face_map)
     bottom = lax.broadcasted_iota(jnp.int32, main.shape, 1) == 0
     return jnp.where(bottom, main + add[:, None, :], main)

time: 51.8 us -> 48.3 us (0.932)
  local copies, waits for them, and re-layouts: 5.44 us -> 0 us
  Pallas kernels: 45 us -> 46.1 us
  other arithmetic: 1.01 us -> 2.09 us
    unnamed x20 -> x0, local copies, waits for them, and re-layouts: 5.44 us -> none
    select_n x1, other arithmetic: 1 us -> 2.09 us  [shards(): return jnp.where(bottom, main + add[:, None, :], main)]
    pallas_call x1, Pallas kernels: 45 us -> 46.1 us  [shards(): pl.pallas_call(functools.partial(step_kernel, n_blk, n_pair, own, piv, he...]
where the time goes in v2:
time: 48.3 us; the launch traced here: 48.2 us
  Pallas kernels  46.1 us (95%)
  other arithmetic  2.09 us (4%)
    pallas_call x1, Pallas kernels, shards(): pl.pallas_call(functools.partial(step_kernel, n_blk, n_pair, own, piv, he...  46.1 us
    select_n x1, other arithmetic, shards(): return jnp.where(bottom, main + add[:, None, :], main)  2.09 us

profile of v2, /device:TPU:1, one launch (start us, length us, event | category | flops | bytes accessed | tf_op | source)
XLA Modules:
  0.0 48.2 jit_solution(11027885562909734686)
XLA Ops:
  0.0 46.1 %shard_map.100 = (f32[20,32,256]{2,1,0:T(8,128)}, f32[20,256]{1,0:T(8,128)}) custom-call(f32[20,32,256]{2,1,0:T(8,128)} %density.1, f32[160,160]{1,0:T(8,128)} %agg_h.1, f32[160,160]{1,0:T(8,128)} %share_h.1, s32[160,160]{1,0:T(8,128)} %target_h.1, f32[160,160]{1,0:T(8,128)} %frag_h.1, f32[1,160]{1,0:T(1,128)} %bitcast.2, f32[1,160]{1,0:T(1,128)} %bitcast.3, ...), custom_call_target="tpu_custom_call" | custom-call | tf_op jit(solution)/shard_map/pallas_call | solution.py:241
  46.1 2.1 %add_select_fusion = f32[20,32,256]{2,1,0:T(8,128)} fusion(f32[20,32,256]{2,1,0:T(8,128)} %get-tuple-element.7, f32[20,256]{1,0:T(8,128)} %get-tuple-element.8, pred[32]{0:T(512)(128)(4,1)S(1)} %iota_compare_fusion), kind=kLoop, calls=%fused_computation | loop fusion | flops 327680 | bytes 1331232 | tf_op jit(solution)/shard_map/jit(_where)/select_n | solution.py:282
  (1 shorter events, 0.0 us)

commit v3 on v2

v3 whole, which is shorter than its diff:
```python
import functools

import jax
import jax.numpy as jnp
from jax import lax
from jax.experimental import pallas as pl
from jax.experimental.pallas import tpu as pltpu
from jax.sharding import PartitionSpec as P

MESH = pl.DeviceIdType.MESH
BANDS = 5
F32 = jnp.float32
BF16 = jnp.bfloat16
I16 = jnp.int16
RING, CORES = 4, 2
MIDDLE = 1.025
STEP = 1.95 / 65534.0


def permuted(face, one_hot):
    total = None
    for _ in range(3):
        part = face.astype(BF16)
        face = face - part.astype(F32)
        moved = jnp.dot(part, one_hot, preferred_element_type=F32)
        total = moved if total is None else total + moved
    return total


def rounded16(x):
    return jnp.round(x).astype(jnp.int32).astype(I16)


def step_kernel(
    n_pair, own, piv, height, width,
    density, agg_h, share_h, target_h, frag_h, rate, cour, rows_sm, up_sm, face_map,
    main,
    agg, share, target, frag, dens_v, enc, got, v0, sec, res, out_f, out_s, out_r, wb, y_s,
    ring, picked, picked_r, ring2, picked2, picked2_r,
    halo_s, halo_r, halo_c, inflow_s, inflow_r, edge_r, top_s, top_p, top_r, scale_p, scale_r,
    local_sem, main_send, main_recv, halo_send, halo_recv, inflow_send, inflow_recv,
    ring_send, ring_recv, pick_send, pick_recv, ring2_send, ring2_recv, pick2_send, pick2_recv,
    edge_send, edge_recv, top_send, top_recv, out_send, out_recv, scale_send, scale_recv,
):
    me_b, me_p = lax.axis_index("blk"), lax.axis_index("pair")
    grp = me_p // 2
    z_hi, y, core = me_b // (RING * CORES), (me_b // CORES) % RING, me_b % CORES
    pairs = [(me_p + d) % n_pair for d in range(n_pair)]

    def block_at(dz, dy, dc):
        return ((z_hi + dz) % 2) * (RING * CORES) + ((y + dy) % RING) * CORES + (core + dc) % CORES

    ring_mates = [block_at(0, d, 0) for d in range(RING)]
    pick_mates = [block_at(q // 2, 0, q % 2) for q in range(4)]

    loads = [pltpu.make_async_copy(density.at[:, :, pl.ds(t * 128, 128)], dens_v.at[t], local_sem.at[t])
             for t in range(2)]
    for load in loads:
        load.start()
    tables = [pltpu.make_async_copy(src, dst, local_sem.at[2 + n]) for n, (src, dst) in enumerate(
        ((agg_h, agg), (share_h, share), (target_h, target), (frag_h, frag)))]
    for load in tables:
        load.start()

    barrier = pltpu.get_barrier_semaphore()
    for p in pairs[1:]:
        pl.semaphore_signal(barrier, inc=1, device_id=(me_b, p), device_id_type=MESH)
    for b in ring_mates[1:] + pick_mates[1:]:
        pl.semaphore_signal(barrier, inc=1, device_id=(b, me_p), device_id_type=MESH)

    def to_pair(d, src, dst, send, recv):
        return pltpu.make_async_remote_copy(
            src_ref=src, dst_ref=dst, send_sem=send.at[d], recv_sem=recv.at[d],
            device_id=(me_b, pairs[d]), device_id_type=MESH)

    def to_block(b, d, src, dst, send, recv):
        return pltpu.make_async_remote_copy(
            src_ref=src, dst_ref=dst, send_sem=send.at[d], recv_sem=recv.at[d],
            device_id=(b, me_p), device_id_type=MESH)

    live_rows = rows_sm[me_b]
    top_row = live_rows - 1
    for load in loads:
        load.wait()
    dens_rows = dens_v.reshape(2 * own * height, 128)
    for t in range(2):
        at = t * own * height
        ring[y, :, pl.ds(t * 128, 128)] = dens_rows[pl.ds(jnp.maximum(top_row, 0) + at, own, stride=height), :]
        halo_s[t] = jnp.zeros((own, 128), F32)
        for q in range(1, height // 8):
            halo_s[2 * q + t] = dens_rows[pl.ds(8 * q - 1 + at, own, stride=height), :]
    for p in range(n_pair):
        tile = dens_v[p % 2, :, pl.ds((p // 2) * 8, 8), :].reshape(own * 8, 128)
        enc[p] = rounded16((tile - MIDDLE) * (1.0 / STEP))

    for load in tables:
        load.wait()
    row_id = lax.broadcasted_iota(jnp.int32, (piv, piv), 0)
    col_id = lax.broadcasted_iota(jnp.int32, (piv, piv), 1)
    kern = agg[...]
    part = share[...]
    low = (0.5 * kern * part).astype(BF16).astype(F32)
    high = (0.5 * kern * (1.0 - part)).astype(BF16).astype(F32)
    offset = (target[...] - jnp.maximum(row_id, col_id)).astype(F32)
    last = []
    for n, (lo, hi, off, keep) in enumerate((
        (low, high, offset, col_id <= row_id),
        (low.T, high.T, offset.T, col_id < row_id),
    )):
        for d in range(BANDS):
            band = jnp.where(off == d, lo, jnp.where(off == d - 1, hi, 0.0))
            wb[pl.ds((n * BANDS + d) * piv, piv), :] = jnp.where(keep, band, 0.0).astype(BF16)
        last.append(pltpu.roll(jnp.where(keep & (off == -1), lo, 0.0)[piv - 8:], 7, 0))
    rate_row = rate[...]
    cour_row = cour[...]
    base = 2 * BANDS * piv
    wb[pl.ds(base, piv), :] = kern.astype(BF16)
    wb[pl.ds(base + 2 * piv, 16), :] = jnp.concatenate(last, axis=0).astype(BF16)
    smaller = (row_id < col_id).astype(F32)
    wb[pl.ds(base + piv, piv), :] = (frag[...] * rate_row * smaller).astype(BF16)
    diag = row_id == col_id
    rate_col = jnp.sum(jnp.where(diag, rate_row, 0.0), axis=1, keepdims=True)
    cour_col = jnp.sum(jnp.where(diag, cour_row, 0.0), axis=1, keepdims=True)
    own_diag = (lax.broadcasted_iota(jnp.int32, (own, piv), 0) + me_p * own
                == lax.broadcasted_iota(jnp.int32, (own, piv), 1))
    own_cour = jnp.sum(jnp.where(own_diag, cour_row, 0.0), axis=1, keepdims=True)
    one_hot = (lax.broadcasted_iota(jnp.int32, (width, width), 0) == face_map[...]).astype(F32).astype(BF16)

    pl.semaphore_wait(barrier, len(pairs) + len(ring_mates) + len(pick_mates) - 3)

    def along_ring(faces, send, recv):
        copies = [to_block(ring_mates[d], d, faces.at[y], faces.at[y], send, recv) for d in range(1, RING)]
        for copy in copies:
            copy.start()
        return copies

    def across(faces, copies, chosen, chosen_r, send, recv):
        for copy in copies:
            copy.wait_recv()
        for q in range(1, 4):
            chosen[q] = faces[(up_sm[pick_mates[q]] // CORES) % RING]
        more = [to_block(pick_mates[q], q, chosen.at[q], chosen_r.at[q], send, recv) for q in range(1, 4)]
        for copy in more:
            copy.start()
        chosen_r[0] = faces[(up_sm[me_b] // CORES) % RING]
        return more

    def arrived(copies, chosen_r):
        for copy in copies:
            copy.wait_recv()
        u = up_sm[me_b]
        q = ((u // (RING * CORES) + z_hi) % 2) * 2 + (u + core) % 2
        return permuted(chosen_r[q], one_hot)

    ring_out = along_ring(ring, ring_send, ring_recv)
    main_in = [to_pair(d, enc.at[pairs[d]], got.at[me_p], main_send, main_recv) for d in range(1, n_pair)]
    halos = [to_pair(d, halo_s.at[pairs[d]], halo_r.at[me_p], halo_send, halo_recv) for d in range(1, n_pair)]
    for copy in main_in + halos:
        copy.start()
    got_own = pltpu.make_async_copy(enc.at[me_p], got.at[me_p], local_sem.at[6])
    got_own.start()
    halo_own = pltpu.make_async_copy(halo_s.at[me_p], halo_r.at[me_p], local_sem.at[7])
    halo_own.start()

    pick_out = across(ring, ring_out, picked, picked_r, pick_send, pick_recv)
    inflow = arrived(pick_out, picked_r)
    for t in range(2):
        inflow_s[t] = inflow[:, t * 128:(t + 1) * 128]

    def inflow_copy(t, source):
        return pltpu.make_async_remote_copy(
            src_ref=inflow_s.at[t], dst_ref=inflow_r.at[source], send_sem=inflow_send.at[t],
            recv_sem=inflow_recv.at[source], device_id=(me_b, t), device_id_type=MESH)

    for t in range(2):
        @pl.when(me_p != t)
        def _():
            inflow_copy(t, me_p).start()

        @pl.when(me_p == t)
        def _():
            inflow_r[t] = inflow_s[t]

    def change(v, prev):
        y_s[...] = jnp.dot(wb[...], v.astype(BF16), preferred_element_type=F32)
        vb = v.astype(BF16).astype(F32)
        below = y_s[pl.ds(base + 2 * piv, 8), :] + y_s[pl.ds(base + 2 * piv + 8, 8), :]
        y_s[pl.ds(base + 2 * piv - 8, 8), :] += below * vb[piv - 1:]
        births = None
        for d in reversed(range(BANDS)):
            here = vb * (y_s[pl.ds(d * piv, piv), :] + y_s[pl.ds((BANDS + d) * piv, piv), :])
            births = here if births is None else here + pltpu.roll(births, 1, 0)
        loss = y_s[pl.ds(base, piv), :]
        gain = y_s[pl.ds(base + piv, piv), :]
        source = births - v * loss + gain - rate_col * v
        return v + (source - cour_col * (v - prev))

    def start_row(s):
        return v0[pl.ds(s, piv, stride=8), :]

    got_own.wait()
    for copy in main_in:
        copy.wait_recv()
    for p in range(n_pair):
        v0[pl.ds(p * own * 8, own * 8), :] = got[p].astype(jnp.int32).astype(F32) * STEP + MIDDLE
    halo_own.wait()
    for copy in halos:
        copy.wait_recv()
    for p in range(n_pair):
        halo_c[pl.ds(p * own, own), :] = halo_r[p]

    top = None
    edge = to_pair(2, sec.at[:, pl.ds(7 * 128, 128)], edge_r, edge_send, edge_recv)
    for it in reversed(range(4)):
        s = 2 * it
        before = halo_c[...] if it == 0 else start_row(s - 1)
        first, second = start_row(s), start_row(s + 1)
        now = change(jnp.concatenate([first, second], axis=1), jnp.concatenate([before, first], axis=1))
        for t in range(2):
            row = grp * 8 + s + t
            piece = jnp.where(row < live_rows, now[:, t * 128:(t + 1) * 128], 0.0)
            sec[:, pl.ds((s + t) * 128, 128)] = piece
            mine = jnp.where(row == top_row, piece, 0.0)
            top = mine if top is None else top + mine
        if it == 3:
            edge.start()

    top_s[...] = top
    for p in range(n_pair):
        top_p[p] = top_s[pl.ds(p * own, own), :]
    tops = [to_pair(d, top_p.at[pairs[d]], top_r.at[me_p], top_send, top_recv) for d in range(1, n_pair)]
    for copy in tops:
        copy.start()
    top_own = pltpu.make_async_copy(top_p.at[me_p], top_r.at[me_p], local_sem.at[8])
    top_own.start()

    biggest = None
    for it in reversed(range(4)):
        s = 2 * it
        if it == 0:
            @pl.when(grp == 0)
            def _():
                for q in range(n_pair):
                    @pl.when(me_p != q)
                    def _():
                        inflow_copy(0, q).wait_recv()

                for p in range(n_pair):
                    halo_c[pl.ds(p * own, own), :] = inflow_r[p]
                sec[:, :128] += cour_col * halo_c[...]

            edge.wait_recv()
            before = jnp.where(grp > 0, edge_r[...], 0.0)
        else:
            before = sec[:, pl.ds((s - 1) * 128, 128)]
        v = sec[:, pl.ds(s * 128, 256)]
        now = change(v, jnp.concatenate([before, v[:, :128]], axis=1))
        for t in range(2):
            row = grp * 8 + s + t
            piece = 0.5 * start_row(s + t) + 0.5 * now[:, t * 128:(t + 1) * 128]
            piece = jnp.where(row < live_rows, piece, 0.0)
            res[:, pl.ds((s + t) * 128, 128)] = piece
            size = jnp.abs(piece)
            biggest = size if biggest is None else jnp.maximum(biggest, size)

    biggest = jnp.max(biggest, axis=1, keepdims=True)
    finer = jnp.where(biggest > 0.0, 32767.0 / biggest, 0.0)
    for s in range(8):
        out_f[pl.ds(s, piv, stride=8), :] = res[:, pl.ds(s * 128, 128)] * finer
    for p in range(n_pair):
        out_s[p] = rounded16(out_f[pl.ds(p * own * 8, own * 8), :])
    outs = [to_pair(d, out_s.at[pairs[d]], out_r.at[me_p], out_send, out_recv) for d in range(1, n_pair)]
    for copy in outs:
        copy.start()
    top_s[...] = jnp.broadcast_to(biggest * (1.0 / 32767.0), (piv, 128))
    for p in range(n_pair):
        scale_p[p] = top_s[pl.ds(p * own, own), :]
    scales = [to_pair(d, scale_p.at[pairs[d]], scale_r.at[me_p], scale_send, scale_recv) for d in range(1, n_pair)]
    for copy in scales:
        copy.start()
    out_own = [pltpu.make_async_copy(out_s.at[me_p], out_r.at[me_p], local_sem.at[9]),
               pltpu.make_async_copy(scale_p.at[me_p], scale_r.at[me_p], local_sem.at[10])]
    for copy in out_own:
        copy.start()

    top_own.wait()
    for copy in tops:
        copy.wait_recv()
    for t in range(2):
        face = (top_r[t] + top_r[t + 2]) + (top_r[t + 4] + top_r[t + 6])
        ring2[y, :, pl.ds(t * 128, 128)] = face + jnp.where(top_row == 0, own_cour * inflow_s[t], 0.0)
    ring2_out = along_ring(ring2, ring2_send, ring2_recv)
    pick2_out = across(ring2, ring2_out, picked2, picked2_r, pick2_send, pick2_recv)
    add = 0.5 * own_cour * arrived(pick2_out, picked2_r)

    for copy in out_own:
        copy.wait()
    for copy in outs + scales:
        copy.wait_recv()
    bottom = lax.broadcasted_iota(jnp.int32, (own, 8, 128), 1) == 0
    for p in range(n_pair):
        tile = out_r[p].astype(jnp.int32).astype(F32).reshape(own, 8, 128) * scale_r[p][:, None, :]
        if p < 2:
            tile = tile + jnp.where(bottom, add[:, p * 128:(p + 1) * 128][:, None, :], 0.0)
        main[:, pl.ds((p // 2) * 8, 8), pl.ds((p % 2) * 128, 128)] = tile

    for copy in (ring_out + main_in + halos + pick_out + [edge] + tops + outs + scales + ring2_out + pick2_out):
        copy.wait_send()
    for t in range(2):
        @pl.when(me_p != t)
        def _():
            inflow_copy(t, me_p).wait_send()


def shards(n_pair, density, agg, share, target, frag, rate, cour, block_rows, upstream, face_map):
    own, height, width = density.shape
    piv = agg.shape[0]
    vmem = pl.BlockSpec(memory_space=pltpu.VMEM)
    smem = pl.BlockSpec(memory_space=pltpu.SMEM)
    hbm = pl.BlockSpec(memory_space=pltpu.HBM)
    dma = pltpu.SemaphoreType.DMA
    weight_rows = (2 * BANDS + 2) * piv + 16
    return pl.pallas_call(
        functools.partial(step_kernel, n_pair, own, piv, height, width),
        out_shape=jax.ShapeDtypeStruct(density.shape, F32),
        in_specs=[hbm] * 5 + [vmem] * 2 + [smem] * 2 + [vmem],
        out_specs=vmem,
        scratch_shapes=[
            pltpu.VMEM((piv, piv), F32),
            pltpu.VMEM((piv, piv), F32),
            pltpu.VMEM((piv, piv), jnp.int32),
            pltpu.VMEM((piv, piv), F32),
            pltpu.VMEM((2, own, height, 128), F32),
            pltpu.VMEM((n_pair, own * 8, 128), I16),
            pltpu.VMEM((n_pair, own * 8, 128), I16),
            pltpu.VMEM((piv * 8, 128), F32),
            pltpu.VMEM((piv, 1024), F32),
            pltpu.VMEM((piv, 1024), F32),
            pltpu.VMEM((piv * 8, 128), F32),
            pltpu.VMEM((n_pair, own * 8, 128), I16),
            pltpu.VMEM((n_pair, own * 8, 128), I16),
            pltpu.VMEM((weight_rows, piv), BF16),
            pltpu.VMEM((weight_rows, 256), F32),
            pltpu.VMEM((RING, own, width), F32),
            pltpu.VMEM((4, own, width), F32),
            pltpu.VMEM((4, own, width), F32),
            pltpu.VMEM((RING, own, width), F32),
            pltpu.VMEM((4, own, width), F32),
            pltpu.VMEM((4, own, width), F32),
            pltpu.VMEM((n_pair, own, 128), F32),
            pltpu.VMEM((n_pair, own, 128), F32),
            pltpu.VMEM((piv, 128), F32),
            pltpu.VMEM((2, own, 128), F32),
            pltpu.VMEM((n_pair, own, 128), F32),
            pltpu.VMEM((piv, 128), F32),
            pltpu.VMEM((piv, 128), F32),
            pltpu.VMEM((n_pair, own, 128), F32),
            pltpu.VMEM((n_pair, own, 128), F32),
            pltpu.VMEM((n_pair, own, 128), F32),
            pltpu.VMEM((n_pair, own, 128), F32),
            dma((11,)),
            dma((n_pair,)), dma((n_pair,)),
            dma((n_pair,)), dma((n_pair,)),
            dma((2,)), dma((n_pair,)),
            dma((RING,)), dma((RING,)),
            dma((4,)), dma((4,)),
            dma((RING,)), dma((RING,)),
            dma((4,)), dma((4,)),
            dma((n_pair,)), dma((n_pair,)),
            dma((n_pair,)), dma((n_pair,)),
            dma((n_pair,)), dma((n_pair,)),
            dma((n_pair,)), dma((n_pair,)),
        ],
        compiler_params=pltpu.CompilerParams(
            collective_id=0, has_side_effects=True, vmem_limit_bytes=56 * 1024 * 1024),
    )(density, agg, share, target, frag, rate.reshape(1, piv), cour.reshape(1, piv), block_rows, upstream, face_map)


def solution(mesh):
    in_specs = (P("pair", "blk", None), P(), P(), P(), P(), P(), P(), P(), P(), P("blk", None))
    out_specs = P("pair", "blk", None)
    return jax.shard_map(
        functools.partial(shards, mesh.shape["pair"]),
        mesh=mesh, in_specs=in_specs, out_specs=out_specs, check_vma=False)
```

time: 48.3 us -> 36.3 us (0.75)
  Pallas kernels: 46.1 us -> 34.1 us
  other arithmetic: 2.09 us -> 0 us
  local copies, waits for them, and re-layouts: 0 us -> 1.99 us
    pallas_call x1, Pallas kernels: 46.1 us -> 34.1 us  [shards(): pl.pallas_call(functools.partial(step_kernel, n_pair, own, piv, height, w...]
    select_n x1 -> x0, other arithmetic: 2.09 us -> none  [shards(): return jnp.where(bottom, main + add[:, None, :], main)]
    unnamed x0 -> x1, local copies, waits for them, and re-layouts: none -> 1.99 us
where the time goes in v3:
time: 36.3 us; the launch traced here: 36.1 us
  Pallas kernels  34.1 us (94%)
  local copies, waits for them, and re-layouts  1.99 us (5%)
    pallas_call x1, Pallas kernels, shards(): pl.pallas_call(functools.partial(step_kernel, n_pair, own, piv, height, w...  34.1 us
    unnamed x1, local copies, waits for them, and re-layouts  1.99 us

profile of v3, /device:TPU:1, one launch (start us, length us, event | category | flops | bytes accessed | tf_op | source)
XLA Modules:
  0.0 36.1 jit_solution(6498861017017241946)
XLA Ops:
  0.0 34.1 %shard_map.100 = f32[20,32,256]{2,1,0:T(8,128)} custom-call(f32[20,32,256]{2,1,0:T(8,128)} %density.1, f32[160,160]{1,0:T(8,128)} %agg_h.1, f32[160,160]{1,0:T(8,128)} %share_h.1, s32[160,160]{1,0:T(8,128)} %target_h.1, f32[160,160]{1,0:T(8,128)} %frag_h.1, f32[1,160]{1,0:T(1,128)} %bitcast.2, f32[1,160]{1,0:T(1,128)} %bitcast.3, s32[16]{0:T(128)} %rows_sm.1, ...), custom_call_target="tpu_custom_call" | custom-call | tf_op jit(solution)/shard_map/pallas_call | solution.py:323
  34.1 2.0 %copy.12 = f32[20,32,256]{2,1,0:T(8,128)} copy(f32[20,32,256]{2,1,0:T(8,128)} %shard_map.100) | data formatting | bytes 1310720

commit v4 on v3

--- a/solution.py
+++ b/solution.py
@@ -13,6 +13,7 @@
 BF16 = jnp.bfloat16
 I16 = jnp.int16
 RING, CORES = 4, 2
+ORDER = (4, 3, 5, 2, 6, 1, 7)
 MIDDLE = 1.025
 STEP = 1.95 / 65534.0
 
@@ -34,11 +35,11 @@
 def step_kernel(
     n_pair, own, piv, height, width,
     density, agg_h, share_h, target_h, frag_h, rate, cour, rows_sm, up_sm, face_map,
-    main,
-    agg, share, target, frag, dens_v, enc, got, v0, sec, res, out_f, out_s, out_r, wb, y_s,
+    main, add_0, add_1,
+    agg, share, target, frag, dens_v, enc, got, v0, sec, res, out_f, out_s, out_r, main_v, wb, y_s,
     ring, picked, picked_r, ring2, picked2, picked2_r,
-    halo_s, halo_r, halo_c, inflow_s, inflow_r, edge_r, top_s, top_p, top_r, scale_p, scale_r,
-    local_sem, main_send, main_recv, halo_send, halo_recv, inflow_send, inflow_recv,
+    halo_f, halo_c, inflow_s, inflow_r, late_s, late_p, late_r, edge_r, top_s, top_p, top_r, scale_p, scale_r,
+    local_sem, main_send, main_recv, inflow_send, inflow_recv, late_send, late_recv,
     ring_send, ring_recv, pick_send, pick_recv, ring2_send, ring2_recv, pick2_send, pick2_recv,
     edge_send, edge_recv, top_send, top_recv, out_send, out_recv, scale_send, scale_recv,
 ):
@@ -52,6 +53,12 @@
 
     ring_mates = [block_at(0, d, 0) for d in range(RING)]
     pick_mates = [block_at(q // 2, 0, q % 2) for q in range(4)]
+
+    barrier = pltpu.get_barrier_semaphore()
+    for p in pairs[1:]:
+        pl.semaphore_signal(barrier, inc=1, device_id=(me_b, p), device_id_type=MESH)
+    for b in ring_mates[1:] + pick_mates[1:]:
+        pl.semaphore_signal(barrier, inc=1, device_id=(b, me_p), device_id_type=MESH)
 
     loads = [pltpu.make_async_copy(density.at[:, :, pl.ds(t * 128, 128)], dens_v.at[t], local_sem.at[t])
              for t in range(2)]
@@ -62,12 +69,6 @@
     for load in tables:
         load.start()
 
-    barrier = pltpu.get_barrier_semaphore()
-    for p in pairs[1:]:
-        pl.semaphore_signal(barrier, inc=1, device_id=(me_b, p), device_id_type=MESH)
-    for b in ring_mates[1:] + pick_mates[1:]:
-        pl.semaphore_signal(barrier, inc=1, device_id=(b, me_p), device_id_type=MESH)
-
     def to_pair(d, src, dst, send, recv):
         return pltpu.make_async_remote_copy(
             src_ref=src, dst_ref=dst, send_sem=send.at[d], recv_sem=recv.at[d],
@@ -78,20 +79,54 @@
             src_ref=src, dst_ref=dst, send_sem=send.at[d], recv_sem=recv.at[d],
             device_id=(b, me_p), device_id_type=MESH)
 
+    def along_ring(faces, send, recv):
+        copies = [to_block(ring_mates[d], d, faces.at[y], faces.at[y], send, recv) for d in range(1, RING)]
+        for copy in copies:
+            copy.start()
+        return copies
+
+    def across(faces, copies, chosen, chosen_r, send, recv):
+        for copy in copies:
+            copy.wait_recv()
+        for q in range(1, 4):
+            chosen[q] = faces[(up_sm[pick_mates[q]] // CORES) % RING]
+        more = [to_block(pick_mates[q], q, chosen.at[q], chosen_r.at[q], send, recv) for q in range(1, 4)]
+        for copy in more:
+            copy.start()
+        chosen_r[0] = faces[(up_sm[me_b] // CORES) % RING]
+        return more
+
+    def arrived(copies, chosen_r):
+        for copy in copies:
+            copy.wait_recv()
+        u = up_sm[me_b]
+        q = ((u // (RING * CORES) + z_hi) % 2) * 2 + (u + core) % 2
+        return permuted(chosen_r[q], one_hot)
+
     live_rows = rows_sm[me_b]
     top_row = live_rows - 1
+    halo_f[...] = jnp.zeros(halo_f.shape, F32)
     for load in loads:
         load.wait()
     dens_rows = dens_v.reshape(2 * own * height, 128)
     for t in range(2):
-        at = t * own * height
-        ring[y, :, pl.ds(t * 128, 128)] = dens_rows[pl.ds(jnp.maximum(top_row, 0) + at, own, stride=height), :]
-        halo_s[t] = jnp.zeros((own, 128), F32)
-        for q in range(1, height // 8):
-            halo_s[2 * q + t] = dens_rows[pl.ds(8 * q - 1 + at, own, stride=height), :]
-    for p in range(n_pair):
-        tile = dens_v[p % 2, :, pl.ds((p // 2) * 8, 8), :].reshape(own * 8, 128)
-        enc[p] = rounded16((tile - MIDDLE) * (1.0 / STEP))
+        ring[y, :, pl.ds(t * 128, 128)] = dens_rows[
+            pl.ds(jnp.maximum(top_row, 0) + t * own * height, own, stride=height), :]
+    pl.semaphore_wait(barrier, len(pairs) + len(ring_mates) + len(pick_mates) - 3)
+    ring_out = along_ring(ring, ring_send, ring_recv)
+
+    main_in = []
+    for d in ORDER + (0,):
+        p = pairs[d]
+        tile = dens_v[p % 2, :, pl.ds(pl.multiple_of((p // 2) * 8, 8), 8), :].reshape(own * 8, 128)
+        under = jnp.maximum((p // 2) * 8 - 1, 0) + (p % 2) * own * height
+        halo_f[pl.ds(0, own), :] = dens_rows[pl.ds(under, own, stride=height), :]
+        goal = enc.at[d] if d else got.at[me_p]
+        goal[pl.ds(0, own * 8), :] = rounded16((tile - MIDDLE) * (1.0 / STEP))
+        goal[pl.ds(own * 8, 32), :] = rounded16((halo_f[...] - MIDDLE) * (1.0 / STEP))
+        if d:
+            main_in.append(to_pair(d, enc.at[d], got.at[me_p], main_send, main_recv))
+            main_in[-1].start()
 
     for load in tables:
         load.wait()
@@ -126,60 +161,7 @@
     own_cour = jnp.sum(jnp.where(own_diag, cour_row, 0.0), axis=1, keepdims=True)
     one_hot = (lax.broadcasted_iota(jnp.int32, (width, width), 0) == face_map[...]).astype(F32).astype(BF16)
 
-    pl.semaphore_wait(barrier, len(pairs) + len(ring_mates) + len(pick_mates) - 3)
-
-    def along_ring(faces, send, recv):
-        copies = [to_block(ring_mates[d], d, faces.at[y], faces.at[y], send, recv) for d in range(1, RING)]
-        for copy in copies:
-            copy.start()
-        return copies
-
-    def across(faces, copies, chosen, chosen_r, send, recv):
-        for copy in copies:
-            copy.wait_recv()
-        for q in range(1, 4):
-            chosen[q] = faces[(up_sm[pick_mates[q]] // CORES) % RING]
-        more = [to_block(pick_mates[q], q, chosen.at[q], chosen_r.at[q], send, recv) for q in range(1, 4)]
-        for copy in more:
-            copy.start()
-        chosen_r[0] = faces[(up_sm[me_b] // CORES) % RING]
-        return more
-
-    def arrived(copies, chosen_r):
-        for copy in copies:
-            copy.wait_recv()
-        u = up_sm[me_b]
-        q = ((u // (RING * CORES) + z_hi) % 2) * 2 + (u + core) % 2
-        return permuted(chosen_r[q], one_hot)
-
-    ring_out = along_ring(ring, ring_send, ring_recv)
-    main_in = [to_pair(d, enc.at[pairs[d]], got.at[me_p], main_send, main_recv) for d in range(1, n_pair)]
-    halos = [to_pair(d, halo_s.at[pairs[d]], halo_r.at[me_p], halo_send, halo_recv) for d in range(1, n_pair)]
-    for copy in main_in + halos:
-        copy.start()
-    got_own = pltpu.make_async_copy(enc.at[me_p], got.at[me_p], local_sem.at[6])
-    got_own.start()
-    halo_own = pltpu.make_async_copy(halo_s.at[me_p], halo_r.at[me_p], local_sem.at[7])
-    halo_own.start()
-
     pick_out = across(ring, ring_out, picked, picked_r, pick_send, pick_recv)
-    inflow = arrived(pick_out, picked_r)
-    for t in range(2):
-        inflow_s[t] = inflow[:, t * 128:(t + 1) * 128]
-
-    def inflow_copy(t, source):
-        return pltpu.make_async_remote_copy(
-            src_ref=inflow_s.at[t], dst_ref=inflow_r.at[source], send_sem=inflow_send.at[t],
-            recv_sem=inflow_recv.at[source], device_id=(me_b, t), device_id_type=MESH)
-
-    for t in range(2):
-        @pl.when(me_p != t)
-        def _():
-            inflow_copy(t, me_p).start()
-
-        @pl.when(me_p == t)
-        def _():
-            inflow_r[t] = inflow_s[t]
 
     def change(v, prev):
         y_s[...] = jnp.dot(wb[...], v.astype(BF16), preferred_element_type=F32)
@@ -198,16 +180,13 @@
     def start_row(s):
         return v0[pl.ds(s, piv, stride=8), :]
 
-    got_own.wait()
     for copy in main_in:
         copy.wait_recv()
     for p in range(n_pair):
-        v0[pl.ds(p * own * 8, own * 8), :] = got[p].astype(jnp.int32).astype(F32) * STEP + MIDDLE
-    halo_own.wait()
-    for copy in halos:
-        copy.wait_recv()
-    for p in range(n_pair):
-        halo_c[pl.ds(p * own, own), :] = halo_r[p]
+        v0[pl.ds(p * own * 8, own * 8), :] = (
+            got[p, pl.ds(0, own * 8), :].astype(jnp.int32).astype(F32) * STEP + MIDDLE)
+        under = got[p, pl.ds(own * 8, 32), :].astype(jnp.int32).astype(F32) * STEP + MIDDLE
+        halo_c[pl.ds(p * own, own), :] = jnp.where(grp > 0, under[:own], 0.0)
 
     top = None
     edge = to_pair(2, sec.at[:, pl.ds(7 * 128, 128)], edge_r, edge_send, edge_recv)
@@ -234,32 +213,40 @@
     top_own = pltpu.make_async_copy(top_p.at[me_p], top_r.at[me_p], local_sem.at[8])
     top_own.start()
 
+    inflow = arrived(pick_out, picked_r)
+    for t in range(2):
+        inflow_s[t] = inflow[:, t * 128:(t + 1) * 128]
+
+    def inflow_copy(t, source):
+        return pltpu.make_async_remote_copy(
+            src_ref=inflow_s.at[t], dst_ref=inflow_r.at[source], send_sem=inflow_send.at[t],
+            recv_sem=inflow_recv.at[source], device_id=(me_b, t), device_id_type=MESH)
+
+    for t in range(2):
+        @pl.when(me_p != t)
+        def _():
+            inflow_copy(t, me_p).start()
+
+        @pl.when(me_p == t)
+        def _():
+            inflow_r[t] = inflow_s[t]
+
+    def final_rows(it, before):
+        v = sec[:, pl.ds(it * 256, 256)]
+        now = change(v, jnp.concatenate([before, v[:, :128]], axis=1))
+        return [0.5 * start_row(2 * it + t) + 0.5 * now[:, t * 128:(t + 1) * 128] for t in range(2)]
+
     biggest = None
     for it in reversed(range(4)):
-        s = 2 * it
         if it == 0:
-            @pl.when(grp == 0)
-            def _():
-                for q in range(n_pair):
-                    @pl.when(me_p != q)
-                    def _():
-                        inflow_copy(0, q).wait_recv()
-
-                for p in range(n_pair):
-                    halo_c[pl.ds(p * own, own), :] = inflow_r[p]
-                sec[:, :128] += cour_col * halo_c[...]
-
             edge.wait_recv()
-            before = jnp.where(grp > 0, edge_r[...], 0.0)
+            before = edge_r[...]
         else:
-            before = sec[:, pl.ds((s - 1) * 128, 128)]
-        v = sec[:, pl.ds(s * 128, 256)]
-        now = change(v, jnp.concatenate([before, v[:, :128]], axis=1))
-        for t in range(2):
-            row = grp * 8 + s + t
-            piece = 0.5 * start_row(s + t) + 0.5 * now[:, t * 128:(t + 1) * 128]
-            piece = jnp.where(row < live_rows, piece, 0.0)
-            res[:, pl.ds((s + t) * 128, 128)] = piece
+            before = sec[:, pl.ds((2 * it - 1) * 128, 128)]
+        for t, piece in enumerate(final_rows(it, before)):
+            row = grp * 8 + 2 * it + t
+            piece = jnp.where((row < live_rows) & (row >= 2), piece, 0.0)
+            res[:, pl.ds((2 * it + t) * 128, 128)] = piece
             size = jnp.abs(piece)
             biggest = size if biggest is None else jnp.maximum(biggest, size)
 
@@ -290,26 +277,70 @@
         face = (top_r[t] + top_r[t + 2]) + (top_r[t + 4] + top_r[t + 6])
         ring2[y, :, pl.ds(t * 128, 128)] = face + jnp.where(top_row == 0, own_cour * inflow_s[t], 0.0)
     ring2_out = along_ring(ring2, ring2_send, ring2_recv)
+
+    def late_copy(p, source):
+        return pltpu.make_async_remote_copy(
+            src_ref=late_p.at[p], dst_ref=late_r.at[source], send_sem=late_send.at[p],
+            recv_sem=late_recv.at[source], device_id=(me_b, p), device_id_type=MESH)
+
+    @pl.when(grp == 0)
+    def _():
+        for q in range(n_pair):
+            @pl.when(me_p != q)
+            def _():
+                inflow_copy(0, q).wait_recv()
+
+        for p in range(n_pair):
+            halo_c[pl.ds(p * own, own), :] = inflow_r[p]
+        sec[:, :128] += cour_col * halo_c[...]
+        for t, piece in enumerate(final_rows(0, jnp.zeros((piv, 128), F32))):
+            late_s[:, pl.ds(t * 128, 128)] = jnp.where(t < live_rows, piece, 0.0)
+        for p in range(n_pair):
+            late_p[p] = late_s[pl.ds(p * own, own), :]
+        for p in range(n_pair):
+            @pl.when(me_p != p)
+            def _():
+                late_copy(p, me_p).start()
+
+            @pl.when(me_p == p)
+            def _():
+                late_r[min(p, 1)] = late_p[p]
+
     pick2_out = across(ring2, ring2_out, picked2, picked2_r, pick2_send, pick2_recv)
-    add = 0.5 * own_cour * arrived(pick2_out, picked2_r)
 
     for copy in out_own:
         copy.wait()
     for copy in outs + scales:
         copy.wait_recv()
-    bottom = lax.broadcasted_iota(jnp.int32, (own, 8, 128), 1) == 0
     for p in range(n_pair):
         tile = out_r[p].astype(jnp.int32).astype(F32).reshape(own, 8, 128) * scale_r[p][:, None, :]
-        if p < 2:
-            tile = tile + jnp.where(bottom, add[:, p * 128:(p + 1) * 128][:, None, :], 0.0)
-        main[:, pl.ds((p // 2) * 8, 8), pl.ds((p % 2) * 128, 128)] = tile
-
-    for copy in (ring_out + main_in + halos + pick_out + [edge] + tops + outs + scales + ring2_out + pick2_out):
+        main_v[:, pl.ds((p // 2) * 8, 8), pl.ds((p % 2) * 128, 128)] = tile
+    store = pltpu.make_async_copy(main_v, main, local_sem.at[6])
+    store.start()
+
+    for q in range(2):
+        @pl.when(me_p != q)
+        def _():
+            late_copy(0, q).wait_recv()
+    for t, add in enumerate((add_0, add_1)):
+        for q in range(2):
+            add[:, pl.ds(q * 128, 128)] = late_r[q, :, pl.ds(t * 128, 128)]
+    add_0[...] += 0.5 * own_cour * arrived(pick2_out, picked2_r)
+
+    store.wait()
+    for copy in (ring_out + main_in + pick_out + [edge] + tops + outs + scales + ring2_out + pick2_out):
         copy.wait_send()
     for t in range(2):
         @pl.when(me_p != t)
         def _():
             inflow_copy(t, me_p).wait_send()
+
+    @pl.when(grp == 0)
+    def _():
+        for p in range(n_pair):
+            @pl.when(me_p != p)
+            def _():
+                late_copy(p, me_p).wait_send()
 
 
 def shards(n_pair, density, agg, share, target, frag, rate, cour, block_rows, upstream, face_map):
@@ -320,25 +351,30 @@
     hbm = pl.BlockSpec(memory_space=pltpu.HBM)
     dma = pltpu.SemaphoreType.DMA
     weight_rows = (2 * BANDS + 2) * piv + 16
-    return pl.pallas_call(
+    main, add_0, add_1 = pl.pallas_call(
         functools.partial(step_kernel, n_pair, own, piv, height, width),
-        out_shape=jax.ShapeDtypeStruct(density.shape, F32),
+        out_shape=(
+            jax.ShapeDtypeStruct(density.shape, F32),
+            jax.ShapeDtypeStruct((own, width), F32),
+            jax.ShapeDtypeStruct((own, width), F32),
+        ),
         in_specs=[hbm] * 5 + [vmem] * 2 + [smem] * 2 + [vmem],
-        out_specs=vmem,
+        out_specs=(hbm, vmem, vmem),
         scratch_shapes=[
             pltpu.VMEM((piv, piv), F32),
             pltpu.VMEM((piv, piv), F32),
             pltpu.VMEM((piv, piv), jnp.int32),
             pltpu.VMEM((piv, piv), F32),
             pltpu.VMEM((2, own, height, 128), F32),
-            pltpu.VMEM((n_pair, own * 8, 128), I16),
-            pltpu.VMEM((n_pair, own * 8, 128), I16),
+            pltpu.VMEM((n_pair, own * 8 + 32, 128), I16),
+            pltpu.VMEM((n_pair, own * 8 + 32, 128), I16),
             pltpu.VMEM((piv * 8, 128), F32),
             pltpu.VMEM((piv, 1024), F32),
             pltpu.VMEM((piv, 1024), F32),
             pltpu.VMEM((piv * 8, 128), F32),
             pltpu.VMEM((n_pair, own * 8, 128), I16),
             pltpu.VMEM((n_pair, own * 8, 128), I16),
+            pltpu.VMEM((own, height, width), F32),
             pltpu.VMEM((weight_rows, piv), BF16),
             pltpu.VMEM((weight_rows, 256), F32),
             pltpu.VMEM((RING, own, width), F32),
@@ -347,11 +383,13 @@
             pltpu.VMEM((RING, own, width), F32),
             pltpu.VMEM((4, own, width), F32),
             pltpu.VMEM((4, own, width), F32),
-            pltpu.VMEM((n_pair, own, 128), F32),
-            pltpu.VMEM((n_pair, own, 128), F32),
+            pltpu.VMEM((32, 128), F32),
             pltpu.VMEM((piv, 128), F32),
             pltpu.VMEM((2, own, 128), F32),
             pltpu.VMEM((n_pair, own, 128), F32),
+            pltpu.VMEM((piv, 256), F32),
+            pltpu.VMEM((n_pair, own, 256), F32),
+            pltpu.VMEM((2, own, 256), F32),
             pltpu.VMEM((piv, 128), F32),
             pltpu.VMEM((piv, 128), F32),
             pltpu.VMEM((n_pair, own, 128), F32),
@@ -360,8 +398,8 @@
             pltpu.VMEM((n_pair, own, 128), F32),
             dma((11,)),
             dma((n_pair,)), dma((n_pair,)),
-            dma((n_pair,)), dma((n_pair,)),
             dma((2,)), dma((n_pair,)),
+            dma((n_pair,)), dma((2,)),
             dma((RING,)), dma((RING,)),
             dma((4,)), dma((4,)),
             dma((RING,)), dma((RING,)),
@@ -374,6 +412,8 @@
         compiler_params=pltpu.CompilerParams(
             collective_id=0, has_side_effects=True, vmem_limit_bytes=56 * 1024 * 1024),
     )(density, agg, share, target, frag, rate.reshape(1, piv), cour.reshape(1, piv), block_rows, upstream, face_map)
+    row = lax.broadcasted_iota(jnp.int32, main.shape, 1)
+    return main + jnp.where(row == 0, add_0[:, None, :], jnp.where(row == 1, add_1[:, None, :], 0.0))
 
 
 def solution(mesh):

time: 36.3 us -> 35.2 us (0.970)
  other arithmetic: 0 us -> 2.11 us
  local copies, waits for them, and re-layouts: 1.99 us -> 0 us
  Pallas kernels: 34.1 us -> 32.9 us
    add x0 -> x1, other arithmetic: none -> 2.1 us  [shards(): main + jnp.where(row == 0, add_0[:, None, :], jnp.where(row == 1, add_1[:...]
    unnamed x1 -> x0, local copies, waits for them, and re-layouts: 1.99 us -> none
    pallas_call x1, Pallas kernels: 34.1 us -> 32.9 us  [shards(): pl.pallas_call(functools.partial(step_kernel, n_pair, own, piv, height, w...]
where the time goes in v4:
time: 35.2 us; the launch traced here: 35 us
  Pallas kernels  32.9 us (93%)
  other arithmetic  2.11 us (6%)
    pallas_call x1, Pallas kernels, shards(): pl.pallas_call(functools.partial(step_kernel, n_pair, own, piv, height, w...  32.9 us
    add x1, other arithmetic, shards(): main + jnp.where(row == 0, add_0[:, None, :], jnp.where(row == 1, add_1[:...  2.1 us

profile of v4, /device:TPU:1, one launch (start us, length us, event | category | flops | bytes accessed | tf_op | source)
XLA Modules:
  0.0 35.0 jit_solution(3839825024880267918)
XLA Ops:
  0.0 32.9 %shard_map.100 = (f32[20,32,256]{2,1,0:T(8,128)}, f32[20,256]{1,0:T(8,128)}, f32[20,256]{1,0:T(8,128)}) custom-call(f32[20,32,256]{2,1,0:T(8,128)} %density.1, f32[160,160]{1,0:T(8,128)} %agg_h.1, f32[160,160]{1,0:T(8,128)} %share_h.1, s32[160,160]{1,0:T(8,128)} %target_h.1, f32[160,160]{1,0:T(8,128)} %frag_h.1, f32[1,160]{1,0:T(1,128)} %bitcast.2, ...), custom_call_target="tpu_custom_call" | custom-call | tf_op jit(solution)/shard_map/pallas_call | solution.py:354
  32.9 2.1 %select_add_fusion = f32[20,32,256]{2,1,0:T(8,128)} fusion(f32[20,32,256]{2,1,0:T(8,128)} %get-tuple-element.8, f32[20,256]{1,0:T(8,128)} %get-tuple-element.10, f32[20,256]{1,0:T(8,128)} %get-tuple-element.9, pred[32]{0:T(512)(128)(4,1)S(1)} %get-tuple-element.11, pred[32]{0:T(512)(128)(4,1)S(1)} %get-tuple-element.12), kind=kLoop, calls=%fused_computation | loop fusion | flops 491520 | bytes 1351744 | tf_op jit(solution)/shard_map/add | solution.py:416
  (1 shorter events, 0.0 us)

commit v5 on v4

--- a/solution.py
+++ b/solution.py
@@ -38,13 +38,13 @@
     main, add_0, add_1,
     agg, share, target, frag, dens_v, enc, got, v0, sec, res, out_f, out_s, out_r, main_v, wb, y_s,
     ring, picked, picked_r, ring2, picked2, picked2_r,
-    halo_f, halo_c, inflow_s, inflow_r, late_s, late_p, late_r, edge_r, top_s, top_p, top_r, scale_p, scale_r,
+    halo_f, halo_c, inflow_s, inflow_r, face, terms_s, late_s, late_p, late_r, edge_r, wide_s, scale_p, scale_r,
     local_sem, main_send, main_recv, inflow_send, inflow_recv, late_send, late_recv,
     ring_send, ring_recv, pick_send, pick_recv, ring2_send, ring2_recv, pick2_send, pick2_recv,
-    edge_send, edge_recv, top_send, top_recv, out_send, out_recv, scale_send, scale_recv,
+    edge_send, edge_recv, out_send, out_recv, scale_send, scale_recv,
 ):
     me_b, me_p = lax.axis_index("blk"), lax.axis_index("pair")
-    grp = me_p // 2
+    grp, half = me_p // 2, me_p % 2
     z_hi, y, core = me_b // (RING * CORES), (me_b // CORES) % RING, me_b % CORES
     pairs = [(me_p + d) % n_pair for d in range(n_pair)]
 
@@ -159,11 +159,12 @@
     own_diag = (lax.broadcasted_iota(jnp.int32, (own, piv), 0) + me_p * own
                 == lax.broadcasted_iota(jnp.int32, (own, piv), 1))
     own_cour = jnp.sum(jnp.where(own_diag, cour_row, 0.0), axis=1, keepdims=True)
+    own_rate = jnp.sum(jnp.where(own_diag, rate_row, 0.0), axis=1, keepdims=True)
     one_hot = (lax.broadcasted_iota(jnp.int32, (width, width), 0) == face_map[...]).astype(F32).astype(BF16)
 
     pick_out = across(ring, ring_out, picked, picked_r, pick_send, pick_recv)
 
-    def change(v, prev):
+    def mixed(v):
         y_s[...] = jnp.dot(wb[...], v.astype(BF16), preferred_element_type=F32)
         vb = v.astype(BF16).astype(F32)
         below = y_s[pl.ds(base + 2 * piv, 8), :] + y_s[pl.ds(base + 2 * piv + 8, 8), :]
@@ -172,10 +173,10 @@
         for d in reversed(range(BANDS)):
             here = vb * (y_s[pl.ds(d * piv, piv), :] + y_s[pl.ds((BANDS + d) * piv, piv), :])
             births = here if births is None else here + pltpu.roll(births, 1, 0)
-        loss = y_s[pl.ds(base, piv), :]
-        gain = y_s[pl.ds(base + piv, piv), :]
-        source = births - v * loss + gain - rate_col * v
-        return v + (source - cour_col * (v - prev))
+        return births - v * y_s[pl.ds(base, piv), :] + y_s[pl.ds(base + piv, piv), :]
+
+    def change(v, prev):
+        return v + (mixed(v) - rate_col * v - cour_col * (v - prev))
 
     def start_row(s):
         return v0[pl.ds(s, piv, stride=8), :]
@@ -188,7 +189,6 @@
         under = got[p, pl.ds(own * 8, 32), :].astype(jnp.int32).astype(F32) * STEP + MIDDLE
         halo_c[pl.ds(p * own, own), :] = jnp.where(grp > 0, under[:own], 0.0)
 
-    top = None
     edge = to_pair(2, sec.at[:, pl.ds(7 * 128, 128)], edge_r, edge_send, edge_recv)
     for it in reversed(range(4)):
         s = 2 * it
@@ -199,37 +199,23 @@
             row = grp * 8 + s + t
             piece = jnp.where(row < live_rows, now[:, t * 128:(t + 1) * 128], 0.0)
             sec[:, pl.ds((s + t) * 128, 128)] = piece
-            mine = jnp.where(row == top_row, piece, 0.0)
-            top = mine if top is None else top + mine
         if it == 3:
             edge.start()
 
-    top_s[...] = top
-    for p in range(n_pair):
-        top_p[p] = top_s[pl.ds(p * own, own), :]
-    tops = [to_pair(d, top_p.at[pairs[d]], top_r.at[me_p], top_send, top_recv) for d in range(1, n_pair)]
-    for copy in tops:
+    inflow = arrived(pick_out, picked_r)
+    inflow_s[...] = inflow
+    inflows = [to_pair(d, inflow_s, inflow_r.at[me_p], inflow_send, inflow_recv) for d in range(1, n_pair)]
+    for copy in inflows:
         copy.start()
-    top_own = pltpu.make_async_copy(top_p.at[me_p], top_r.at[me_p], local_sem.at[8])
-    top_own.start()
-
-    inflow = arrived(pick_out, picked_r)
+    inflow_r[me_p] = inflow
+
     for t in range(2):
-        inflow_s[t] = inflow[:, t * 128:(t + 1) * 128]
-
-    def inflow_copy(t, source):
-        return pltpu.make_async_remote_copy(
-            src_ref=inflow_s.at[t], dst_ref=inflow_r.at[source], send_sem=inflow_send.at[t],
-            recv_sem=inflow_recv.at[source], device_id=(me_b, t), device_id_type=MESH)
-
-    for t in range(2):
-        @pl.when(me_p != t)
-        def _():
-            inflow_copy(t, me_p).start()
-
-        @pl.when(me_p == t)
-        def _():
-            inflow_r[t] = inflow_s[t]
+        cols = pl.ds(t * 128, 128)
+        v = ring[y, :, cols]
+        under = dens_rows[pl.ds(jnp.maximum(top_row - 1, 0) + t * own * height, own, stride=height), :]
+        prev = jnp.where(top_row == 0, inflow[:, t * 128:(t + 1) * 128], under)
+        ring2[y, :, cols] = v - own_cour * (v - prev) - own_rate * v
+    ring2_out = along_ring(ring2, ring2_send, ring2_recv)
 
     def final_rows(it, before):
         v = sec[:, pl.ds(it * 256, 256)]
@@ -259,9 +245,9 @@
     outs = [to_pair(d, out_s.at[pairs[d]], out_r.at[me_p], out_send, out_recv) for d in range(1, n_pair)]
     for copy in outs:
         copy.start()
-    top_s[...] = jnp.broadcast_to(biggest * (1.0 / 32767.0), (piv, 128))
+    wide_s[...] = jnp.broadcast_to(biggest * (1.0 / 32767.0), (piv, 128))
     for p in range(n_pair):
-        scale_p[p] = top_s[pl.ds(p * own, own), :]
+        scale_p[p] = wide_s[pl.ds(p * own, own), :]
     scales = [to_pair(d, scale_p.at[pairs[d]], scale_r.at[me_p], scale_send, scale_recv) for d in range(1, n_pair)]
     for copy in scales:
         copy.start()
@@ -270,13 +256,11 @@
     for copy in out_own:
         copy.start()
 
-    top_own.wait()
-    for copy in tops:
+    pick2_out = across(ring2, ring2_out, picked2, picked2_r, pick2_send, pick2_recv)
+    for copy in inflows:
         copy.wait_recv()
-    for t in range(2):
-        face = (top_r[t] + top_r[t + 2]) + (top_r[t + 4] + top_r[t + 6])
-        ring2[y, :, pl.ds(t * 128, 128)] = face + jnp.where(top_row == 0, own_cour * inflow_s[t], 0.0)
-    ring2_out = along_ring(ring2, ring2_send, ring2_recv)
+    for p in range(n_pair):
+        face[pl.ds(p * own, own), :] = inflow_r[p]
 
     def late_copy(p, source):
         return pltpu.make_async_remote_copy(
@@ -285,14 +269,7 @@
 
     @pl.when(grp == 0)
     def _():
-        for q in range(n_pair):
-            @pl.when(me_p != q)
-            def _():
-                inflow_copy(0, q).wait_recv()
-
-        for p in range(n_pair):
-            halo_c[pl.ds(p * own, own), :] = inflow_r[p]
-        sec[:, :128] += cour_col * halo_c[...]
+        sec[:, :128] += cour_col * jnp.where(half == 0, face[:, :128], face[:, 128:])
         for t, piece in enumerate(final_rows(0, jnp.zeros((piv, 128), F32))):
             late_s[:, pl.ds(t * 128, 128)] = jnp.where(t < live_rows, piece, 0.0)
         for p in range(n_pair):
@@ -306,7 +283,9 @@
             def _():
                 late_r[min(p, 1)] = late_p[p]
 
-    pick2_out = across(ring2, ring2_out, picked2, picked2_r, pick2_send, pick2_recv)
+    terms = mixed(face[...])
+    for t in range(2):
+        terms_s[pl.ds(t, piv, stride=8), :] = terms[:, t * 128:(t + 1) * 128]
 
     for copy in out_own:
         copy.wait()
@@ -325,15 +304,15 @@
     for t, add in enumerate((add_0, add_1)):
         for q in range(2):
             add[:, pl.ds(q * 128, 128)] = late_r[q, :, pl.ds(t * 128, 128)]
-    add_0[...] += 0.5 * own_cour * arrived(pick2_out, picked2_r)
+    linear = arrived(pick2_out, picked2_r)
+    for t in range(2):
+        cols = slice(t * 128, (t + 1) * 128)
+        top = linear[:, cols] + terms_s[pl.ds(me_p * own * 8 + t, own, stride=8), :]
+        add_0[:, cols] += 0.5 * own_cour * top
 
     store.wait()
-    for copy in (ring_out + main_in + pick_out + [edge] + tops + outs + scales + ring2_out + pick2_out):
+    for copy in (ring_out + main_in + pick_out + inflows + [edge] + outs + scales + ring2_out + pick2_out):
         copy.wait_send()
-    for t in range(2):
-        @pl.when(me_p != t)
-        def _():
-            inflow_copy(t, me_p).wait_send()
 
     @pl.when(grp == 0)
     def _():
@@ -385,8 +364,10 @@
             pltpu.VMEM((4, own, width), F32),
             pltpu.VMEM((32, 128), F32),
             pltpu.VMEM((piv, 128), F32),
-            pltpu.VMEM((2, own, 128), F32),
-            pltpu.VMEM((n_pair, own, 128), F32),
+            pltpu.VMEM((own, width), F32),
+            pltpu.VMEM((n_pair, own, width), F32),
+            pltpu.VMEM((piv, width), F32),
+            pltpu.VMEM((piv * 8, 128), F32),
             pltpu.VMEM((piv, 256), F32),
             pltpu.VMEM((n_pair, own, 256), F32),
             pltpu.VMEM((2, own, 256), F32),
@@ -394,17 +375,14 @@
             pltpu.VMEM((piv, 128), F32),
             pltpu.VMEM((n_pair, own, 128), F32),
             pltpu.VMEM((n_pair, own, 128), F32),
-            pltpu.VMEM((n_pair, own, 128), F32),
-            pltpu.VMEM((n_pair, own, 128), F32),
             dma((11,)),
             dma((n_pair,)), dma((n_pair,)),
-            dma((2,)), dma((n_pair,)),
+            dma((n_pair,)), dma((n_pair,)),
             dma((n_pair,)), dma((2,)),
             dma((RING,)), dma((RING,)),
             dma((4,)), dma((4,)),
             dma((RING,)), dma((RING,)),
             dma((4,)), dma((4,)),
-            dma((n_pair,)), dma((n_pair,)),
             dma((n_pair,)), dma((n_pair,)),
             dma((n_pair,)), dma((n_pair,)),
             dma((n_pair,)), dma((n_pair,)),

time: 35.2 us -> 33.1 us (0.940)
  Pallas kernels: 32.9 us -> 30.8 us
    pallas_call x1, Pallas kernels: 32.9 us -> 30.8 us  [shards(): pl.pallas_call(functools.partial(step_kernel, n_pair, own, piv, height, w...]
where the time goes in v5:
time: 33.1 us; the launch traced here: 32.9 us
  Pallas kernels  30.8 us (93%)
  other arithmetic  2.11 us (6%)
    pallas_call x1, Pallas kernels, shards(): pl.pallas_call(functools.partial(step_kernel, n_pair, own, piv, height, w...  30.8 us
    add x1, other arithmetic, shards(): main + jnp.where(row == 0, add_0[:, None, :], jnp.where(row == 1, add_1[:...  2.1 us

profile of v5, /device:TPU:1, one launch (start us, length us, event | category | flops | bytes accessed | tf_op | source)
XLA Modules:
  0.0 32.9 jit_solution(17131572003831627148)
XLA Ops:
  0.0 30.8 %shard_map.100 = (f32[20,32,256]{2,1,0:T(8,128)}, f32[20,256]{1,0:T(8,128)}, f32[20,256]{1,0:T(8,128)}) custom-call(f32[20,32,256]{2,1,0:T(8,128)} %density.1, f32[160,160]{1,0:T(8,128)} %agg_h.1, f32[160,160]{1,0:T(8,128)} %share_h.1, s32[160,160]{1,0:T(8,128)} %target_h.1, f32[160,160]{1,0:T(8,128)} %frag_h.1, f32[1,160]{1,0:T(1,128)} %bitcast.2, ...), custom_call_target="tpu_custom_call" | custom-call | tf_op jit(solution)/shard_map/pallas_call | solution.py:333
  30.8 2.1 %select_add_fusion = f32[20,32,256]{2,1,0:T(8,128)} fusion(f32[20,32,256]{2,1,0:T(8,128)} %get-tuple-element.8, f32[20,256]{1,0:T(8,128)} %get-tuple-element.10, f32[20,256]{1,0:T(8,128)} %get-tuple-element.9, pred[32]{0:T(512)(128)(4,1)S(1)} %get-tuple-element.11, pred[32]{0:T(512)(128)(4,1)S(1)} %get-tuple-element.12), kind=kLoop, calls=%fused_computation | loop fusion | flops 491520 | bytes 1351744 | tf_op jit(solution)/shard_map/add | solution.py:394
  (1 shorter events, 0.0 us)

commit v6 on v5

--- a/solution.py
+++ b/solution.py
@@ -16,6 +16,7 @@
 ORDER = (4, 3, 5, 2, 6, 1, 7)
 MIDDLE = 1.025
 STEP = 1.95 / 65534.0
+LEAST = 32768.0 / 65536.0
 
 
 def permuted(face, one_hot):
@@ -34,14 +35,14 @@
 
 def step_kernel(
     n_pair, own, piv, height, width,
-    density, agg_h, share_h, target_h, frag_h, rate, cour, rows_sm, up_sm, face_map,
+    density, agg_h, share_h, target_h, frag_h, rate_h, cour_h, rows_h, up_h, map_h,
     main, add_0, add_1,
-    agg, share, target, frag, dens_v, enc, got, v0, sec, res, out_f, out_s, out_r, main_v, wb, y_s,
+    agg, share, target, frag, rate, cour, rows_sm, up_sm, face_map, dens_v, enc, got, v0, sec, res, out_f, out_s, out_r, main_v, wb, y_s,
     ring, picked, picked_r, ring2, picked2, picked2_r,
-    halo_f, halo_c, inflow_s, inflow_r, face, terms_s, late_s, late_p, late_r, edge_r, wide_s, scale_p, scale_r,
+    halo_f, halo_c, inflow_s, inflow_r, face, terms_s, late_s, late_p, late_r, edge_r, wide_s,
     local_sem, main_send, main_recv, inflow_send, inflow_recv, late_send, late_recv,
     ring_send, ring_recv, pick_send, pick_recv, ring2_send, ring2_recv, pick2_send, pick2_recv,
-    edge_send, edge_recv, out_send, out_recv, scale_send, scale_recv,
+    edge_send, edge_recv, out_send, out_recv,
 ):
     me_b, me_p = lax.axis_index("blk"), lax.axis_index("pair")
     grp, half = me_p // 2, me_p % 2
@@ -64,8 +65,13 @@
              for t in range(2)]
     for load in loads:
         load.start()
+    scalars = [pltpu.make_async_copy(rows_h, rows_sm, local_sem.at[11]),
+               pltpu.make_async_copy(up_h, up_sm, local_sem.at[12])]
+    for load in scalars:
+        load.start()
     tables = [pltpu.make_async_copy(src, dst, local_sem.at[2 + n]) for n, (src, dst) in enumerate(
-        ((agg_h, agg), (share_h, share), (target_h, target), (frag_h, frag)))]
+        ((agg_h, agg), (share_h, share), (target_h, target), (frag_h, frag),
+         (rate_h, rate), (cour_h, cour), (map_h, face_map)))]
     for load in tables:
         load.start()
 
@@ -103,9 +109,11 @@
         q = ((u // (RING * CORES) + z_hi) % 2) * 2 + (u + core) % 2
         return permuted(chosen_r[q], one_hot)
 
+    halo_f[...] = jnp.zeros(halo_f.shape, F32)
+    for load in scalars:
+        load.wait()
     live_rows = rows_sm[me_b]
     top_row = live_rows - 1
-    halo_f[...] = jnp.zeros(halo_f.shape, F32)
     for load in loads:
         load.wait()
     dens_rows = dens_v.reshape(2 * own * height, 128)
@@ -236,27 +244,28 @@
             size = jnp.abs(piece)
             biggest = size if biggest is None else jnp.maximum(biggest, size)
 
+    pick2_out = across(ring2, ring2_out, picked2, picked2_r, pick2_send, pick2_recv)
+
     biggest = jnp.max(biggest, axis=1, keepdims=True)
     finer = jnp.where(biggest > 0.0, 32767.0 / biggest, 0.0)
     for s in range(8):
         out_f[pl.ds(s, piv, stride=8), :] = res[:, pl.ds(s * 128, 128)] * finer
+    lane = lax.broadcasted_iota(jnp.int32, (piv, 128), 1)
+    wide_s[pl.ds(piv, 16), :] = jnp.zeros((16, 128), F32)
+    first = jnp.floor(biggest * LEAST)
+    rest = (biggest * LEAST - first) * 32768.0
+    second = jnp.floor(rest)
+    third = jnp.floor((rest - second) * 32768.0)
+    wide_s[pl.ds(0, piv), :] = jnp.where(lane == 0, first, jnp.where(lane == 1, second, jnp.where(lane == 2, third, 0.0)))
     for p in range(n_pair):
-        out_s[p] = rounded16(out_f[pl.ds(p * own * 8, own * 8), :])
-    outs = [to_pair(d, out_s.at[pairs[d]], out_r.at[me_p], out_send, out_recv) for d in range(1, n_pair)]
+        out_s[p, pl.ds(0, own * 8), :] = rounded16(out_f[pl.ds(p * own * 8, own * 8), :])
+        out_s[p, pl.ds(own * 8, 32), :] = rounded16(wide_s[pl.ds(p * own, 32), :])
+    outs = [to_pair(d, out_s.at[pairs[d]], out_r.at[me_p], out_send, out_recv) for d in ORDER]
     for copy in outs:
         copy.start()
-    wide_s[...] = jnp.broadcast_to(biggest * (1.0 / 32767.0), (piv, 128))
-    for p in range(n_pair):
-        scale_p[p] = wide_s[pl.ds(p * own, own), :]
-    scales = [to_pair(d, scale_p.at[pairs[d]], scale_r.at[me_p], scale_send, scale_recv) for d in range(1, n_pair)]
-    for copy in scales:
-        copy.start()
-    out_own = [pltpu.make_async_copy(out_s.at[me_p], out_r.at[me_p], local_sem.at[9]),
-               pltpu.make_async_copy(scale_p.at[me_p], scale_r.at[me_p], local_sem.at[10])]
-    for copy in out_own:
-        copy.start()
-
-    pick2_out = across(ring2, ring2_out, picked2, picked2_r, pick2_send, pick2_recv)
+    out_own = pltpu.make_async_copy(out_s.at[me_p], out_r.at[me_p], local_sem.at[9])
+    out_own.start()
+
     for copy in inflows:
         copy.wait_recv()
     for p in range(n_pair):
@@ -287,14 +296,19 @@
     for t in range(2):
         terms_s[pl.ds(t, piv, stride=8), :] = terms[:, t * 128:(t + 1) * 128]
 
-    for copy in out_own:
-        copy.wait()
-    for copy in outs + scales:
+    digit = lax.broadcasted_iota(jnp.int32, (own, 128), 1)
+    digit_size = jnp.where(
+        digit == 0, 1.0, jnp.where(digit == 1, 1.0 / 32768.0, jnp.where(digit == 2, 1.0 / 32768.0 ** 2, 0.0))
+    ) * (1.0 / (LEAST * 32767.0))
+    out_own.wait()
+    for copy in outs:
         copy.wait_recv()
     for p in range(n_pair):
-        tile = out_r[p].astype(jnp.int32).astype(F32).reshape(own, 8, 128) * scale_r[p][:, None, :]
+        digits = out_r[p, pl.ds(own * 8, 32), :].astype(jnp.int32).astype(F32)[:own]
+        scale = jnp.sum(digits * digit_size, axis=1, keepdims=True)
+        tile = out_r[p, pl.ds(0, own * 8), :].astype(jnp.int32).astype(F32).reshape(own, 8, 128) * scale[:, :, None]
         main_v[:, pl.ds((p // 2) * 8, 8), pl.ds((p % 2) * 128, 128)] = tile
-    store = pltpu.make_async_copy(main_v, main, local_sem.at[6])
+    store = pltpu.make_async_copy(main_v, main, local_sem.at[10])
     store.start()
 
     for q in range(2):
@@ -311,7 +325,7 @@
         add_0[:, cols] += 0.5 * own_cour * top
 
     store.wait()
-    for copy in (ring_out + main_in + pick_out + inflows + [edge] + outs + scales + ring2_out + pick2_out):
+    for copy in (ring_out + main_in + pick_out + inflows + [edge] + outs + ring2_out + pick2_out):
         copy.wait_send()
 
     @pl.when(grp == 0)
@@ -326,7 +340,6 @@
     own, height, width = density.shape
     piv = agg.shape[0]
     vmem = pl.BlockSpec(memory_space=pltpu.VMEM)
-    smem = pl.BlockSpec(memory_space=pltpu.SMEM)
     hbm = pl.BlockSpec(memory_space=pltpu.HBM)
     dma = pltpu.SemaphoreType.DMA
     weight_rows = (2 * BANDS + 2) * piv + 16
@@ -337,13 +350,18 @@
             jax.ShapeDtypeStruct((own, width), F32),
             jax.ShapeDtypeStruct((own, width), F32),
         ),
-        in_specs=[hbm] * 5 + [vmem] * 2 + [smem] * 2 + [vmem],
+        in_specs=[hbm] * 10,
         out_specs=(hbm, vmem, vmem),
         scratch_shapes=[
             pltpu.VMEM((piv, piv), F32),
             pltpu.VMEM((piv, piv), F32),
             pltpu.VMEM((piv, piv), jnp.int32),
             pltpu.VMEM((piv, piv), F32),
+            pltpu.VMEM((1, piv), F32),
+            pltpu.VMEM((1, piv), F32),
+            pltpu.SMEM(block_rows.shape, jnp.int32),
+            pltpu.SMEM(upstream.shape, jnp.int32),
+            pltpu.VMEM(face_map.shape, jnp.int32),
             pltpu.VMEM((2, own, height, 128), F32),
             pltpu.VMEM((n_pair, own * 8 + 32, 128), I16),
             pltpu.VMEM((n_pair, own * 8 + 32, 128), I16),
@@ -351,8 +369,8 @@
             pltpu.VMEM((piv, 1024), F32),
             pltpu.VMEM((piv, 1024), F32),
             pltpu.VMEM((piv * 8, 128), F32),
-            pltpu.VMEM((n_pair, own * 8, 128), I16),
-            pltpu.VMEM((n_pair, own * 8, 128), I16),
+            pltpu.VMEM((n_pair, own * 8 + 32, 128), I16),
+            pltpu.VMEM((n_pair, own * 8 + 32, 128), I16),
             pltpu.VMEM((own, height, width), F32),
             pltpu.VMEM((weight_rows, piv), BF16),
             pltpu.VMEM((weight_rows, 256), F32),
@@ -372,10 +390,8 @@
             pltpu.VMEM((n_pair, own, 256), F32),
             pltpu.VMEM((2, own, 256), F32),
             pltpu.VMEM((piv, 128), F32),
-            pltpu.VMEM((piv, 128), F32),
-            pltpu.VMEM((n_pair, own, 128), F32),
-            pltpu.VMEM((n_pair, own, 128), F32),
-            dma((11,)),
+            pltpu.VMEM((piv + 16, 128), F32),
+            dma((13,)),
             dma((n_pair,)), dma((n_pair,)),
             dma((n_pair,)), dma((n_pair,)),
             dma((n_pair,)), dma((2,)),
@@ -385,7 +401,6 @@
             dma((4,)), dma((4,)),
             dma((n_pair,)), dma((n_pair,)),
             dma((n_pair,)), dma((n_pair,)),
-            dma((n_pair,)), dma((n_pair,)),
         ],
         compiler_params=pltpu.CompilerParams(
             collective_id=0, has_side_effects=True, vmem_limit_bytes=56 * 1024 * 1024),

time: 33.1 us -> 31.8 us (0.961)
  Pallas kernels: 30.8 us -> 29.5 us
    pallas_call x1, Pallas kernels: 30.8 us -> 29.5 us  [shards(): pl.pallas_call(functools.partial(step_kernel, n_pair, own, piv, height, w...]
where the time goes in v6:
time: 31.8 us; the launch traced here: 31.6 us
  Pallas kernels  29.5 us (93%)
  other arithmetic  2.11 us (7%)
    pallas_call x1, Pallas kernels, shards(): pl.pallas_call(functools.partial(step_kernel, n_pair, own, piv, height, w...  29.5 us
    add x1, other arithmetic, shards(): main + jnp.where(row == 0, add_0[:, None, :], jnp.where(row == 1, add_1[:...  2.1 us

profile of v6, /device:TPU:1, one launch (start us, length us, event | category | flops | bytes accessed | tf_op | source)
XLA Modules:
  0.0 31.6 jit_solution(6462864939966134067)
XLA Ops:
  0.0 29.5 %shard_map.100 = (f32[20,32,256]{2,1,0:T(8,128)}, f32[20,256]{1,0:T(8,128)}, f32[20,256]{1,0:T(8,128)}) custom-call(f32[20,32,256]{2,1,0:T(8,128)} %density.1, f32[160,160]{1,0:T(8,128)} %agg_h.1, f32[160,160]{1,0:T(8,128)} %share_h.1, s32[160,160]{1,0:T(8,128)} %target_h.1, f32[160,160]{1,0:T(8,128)} %frag_h.1, f32[1,160]{1,0:T(1,128)} %bitcast.2, ...), custom_call_target="tpu_custom_call" | custom-call | tf_op jit(solution)/shard_map/pallas_call | solution.py:346
  29.5 2.1 %select_add_fusion = f32[20,32,256]{2,1,0:T(8,128)} fusion(f32[20,32,256]{2,1,0:T(8,128)} %get-tuple-element.8, f32[20,256]{1,0:T(8,128)} %get-tuple-element.10, f32[20,256]{1,0:T(8,128)} %get-tuple-element.9, pred[32]{0:T(512)(128)(4,1)S(1)} %get-tuple-element.11, pred[32]{0:T(512)(128)(4,1)S(1)} %get-tuple-element.12), kind=kLoop, calls=%fused_computation | loop fusion | flops 491520 | bytes 1351744 | tf_op jit(solution)/shard_map/add | solution.py:409
  (1 shorter events, 0.0 us)

commit v7 on v6

--- a/solution.py
+++ b/solution.py
@@ -37,12 +37,12 @@
     n_pair, own, piv, height, width,
     density, agg_h, share_h, target_h, frag_h, rate_h, cour_h, rows_h, up_h, map_h,
     main, add_0, add_1,
-    agg, share, target, frag, rate, cour, rows_sm, up_sm, face_map, dens_v, enc, got, v0, sec, res, out_f, out_s, out_r, main_v, wb, y_s,
+    agg, share, target, frag, rate, cour, rows_sm, up_sm, face_map, dens_v, enc, got, v0, sec, res, out_f, out_s, out_r, wb, y_s,
     ring, picked, picked_r, ring2, picked2, picked2_r,
-    halo_f, halo_c, inflow_s, inflow_r, face, terms_s, late_s, late_p, late_r, edge_r, wide_s,
+    halo_f, halo_c, inflow_s, inflow_r, face, terms_s, late_s, late_p, late_r, edge, wide_s,
     local_sem, main_send, main_recv, inflow_send, inflow_recv, late_send, late_recv,
     ring_send, ring_recv, pick_send, pick_recv, ring2_send, ring2_recv, pick2_send, pick2_recv,
-    edge_send, edge_recv, out_send, out_recv,
+    out_send, out_recv,
 ):
     me_b, me_p = lax.axis_index("blk"), lax.axis_index("pair")
     grp, half = me_p // 2, me_p % 2
@@ -127,11 +127,12 @@
     for d in ORDER + (0,):
         p = pairs[d]
         tile = dens_v[p % 2, :, pl.ds(pl.multiple_of((p // 2) * 8, 8), 8), :].reshape(own * 8, 128)
-        under = jnp.maximum((p // 2) * 8 - 1, 0) + (p % 2) * own * height
-        halo_f[pl.ds(0, own), :] = dens_rows[pl.ds(under, own, stride=height), :]
+        for n in range(2):
+            under = jnp.maximum((p // 2) * 8 - 1 - n, 0) + (p % 2) * own * height
+            halo_f[pl.ds(n * own, own), :] = dens_rows[pl.ds(under, own, stride=height), :]
         goal = enc.at[d] if d else got.at[me_p]
         goal[pl.ds(0, own * 8), :] = rounded16((tile - MIDDLE) * (1.0 / STEP))
-        goal[pl.ds(own * 8, 32), :] = rounded16((halo_f[...] - MIDDLE) * (1.0 / STEP))
+        goal[pl.ds(own * 8, 48), :] = rounded16((halo_f[...] - MIDDLE) * (1.0 / STEP))
         if d:
             main_in.append(to_pair(d, enc.at[d], got.at[me_p], main_send, main_recv))
             main_in[-1].start()
@@ -145,20 +146,18 @@
     low = (0.5 * kern * part).astype(BF16).astype(F32)
     high = (0.5 * kern * (1.0 - part)).astype(BF16).astype(F32)
     offset = (target[...] - jnp.maximum(row_id, col_id)).astype(F32)
-    last = []
-    for n, (lo, hi, off, keep) in enumerate((
-        (low, high, offset, col_id <= row_id),
-        (low.T, high.T, offset.T, col_id < row_id),
-    )):
-        for d in range(BANDS):
-            band = jnp.where(off == d, lo, jnp.where(off == d - 1, hi, 0.0))
-            wb[pl.ds((n * BANDS + d) * piv, piv), :] = jnp.where(keep, band, 0.0).astype(BF16)
-        last.append(pltpu.roll(jnp.where(keep & (off == -1), lo, 0.0)[piv - 8:], 7, 0))
+    triangles = ((low, high, offset, col_id <= row_id), (low.T, high.T, offset.T, col_id < row_id))
+    for d in range(BANDS):
+        pair = [jnp.where(keep, jnp.where(off == d, lo, jnp.where(off == d - 1, hi, 0.0)), 0.0)
+                for lo, hi, off, keep in triangles]
+        wb[pl.ds(d * piv, piv), :] = (pair[0] + pair[1]).astype(BF16)
+    pair = [jnp.where(keep & (off == -1), lo, 0.0)[piv - 8:] for lo, hi, off, keep in triangles]
+    last = pltpu.roll(pair[0] + pair[1], 7, 0)
     rate_row = rate[...]
     cour_row = cour[...]
-    base = 2 * BANDS * piv
+    base = BANDS * piv
     wb[pl.ds(base, piv), :] = kern.astype(BF16)
-    wb[pl.ds(base + 2 * piv, 16), :] = jnp.concatenate(last, axis=0).astype(BF16)
+    wb[pl.ds(base + 2 * piv, 16), :] = jnp.concatenate([last, jnp.zeros_like(last)], axis=0).astype(BF16)
     smaller = (row_id < col_id).astype(F32)
     wb[pl.ds(base + piv, piv), :] = (frag[...] * rate_row * smaller).astype(BF16)
     diag = row_id == col_id
@@ -173,57 +172,60 @@
     pick_out = across(ring, ring_out, picked, picked_r, pick_send, pick_recv)
 
     def mixed(v):
-        y_s[...] = jnp.dot(wb[...], v.astype(BF16), preferred_element_type=F32)
+        y_s[:, :v.shape[1]] = jnp.dot(wb[...], v.astype(BF16), preferred_element_type=F32)
         vb = v.astype(BF16).astype(F32)
-        below = y_s[pl.ds(base + 2 * piv, 8), :] + y_s[pl.ds(base + 2 * piv + 8, 8), :]
-        y_s[pl.ds(base + 2 * piv - 8, 8), :] += below * vb[piv - 1:]
+        cols = slice(0, v.shape[1])
+        y_s[pl.ds(base + 2 * piv - 8, 8), cols] += y_s[pl.ds(base + 2 * piv, 8), cols] * vb[piv - 1:]
         births = None
         for d in reversed(range(BANDS)):
-            here = vb * (y_s[pl.ds(d * piv, piv), :] + y_s[pl.ds((BANDS + d) * piv, piv), :])
+            here = vb * y_s[pl.ds(d * piv, piv), cols]
             births = here if births is None else here + pltpu.roll(births, 1, 0)
-        return births - v * y_s[pl.ds(base, piv), :] + y_s[pl.ds(base + piv, piv), :]
+        return births - v * y_s[pl.ds(base, piv), cols] + y_s[pl.ds(base + piv, piv), cols]
 
     def change(v, prev):
         return v + (mixed(v) - rate_col * v - cour_col * (v - prev))
 
     def start_row(s):
         return v0[pl.ds(s, piv, stride=8), :]
+
+    def first_inflow():
+        inflow = arrived(pick_out, picked_r)
+        inflow_s[...] = inflow
+        inflows = [to_pair(d, inflow_s, inflow_r.at[me_p], inflow_send, inflow_recv) for d in range(1, n_pair)]
+        for copy in inflows:
+            copy.start()
+        inflow_r[me_p] = inflow
+
+        for t in range(2):
+            cols = pl.ds(t * 128, 128)
+            v = ring[y, :, cols]
+            under = dens_rows[pl.ds(jnp.maximum(top_row - 1, 0) + t * own * height, own, stride=height), :]
+            prev = jnp.where(top_row == 0, inflow[:, t * 128:(t + 1) * 128], under)
+            ring2[y, :, cols] = v - own_cour * (v - prev) - own_rate * v
+        ring2_out = along_ring(ring2, ring2_send, ring2_recv)
+        return inflow, inflows, ring2_out
 
     for copy in main_in:
         copy.wait_recv()
     for p in range(n_pair):
         v0[pl.ds(p * own * 8, own * 8), :] = (
             got[p, pl.ds(0, own * 8), :].astype(jnp.int32).astype(F32) * STEP + MIDDLE)
-        under = got[p, pl.ds(own * 8, 32), :].astype(jnp.int32).astype(F32) * STEP + MIDDLE
-        halo_c[pl.ds(p * own, own), :] = jnp.where(grp > 0, under[:own], 0.0)
-
-    edge = to_pair(2, sec.at[:, pl.ds(7 * 128, 128)], edge_r, edge_send, edge_recv)
+        halo_f[...] = got[p, pl.ds(own * 8, 48), :].astype(jnp.int32).astype(F32) * STEP + MIDDLE
+        for n in range(2):
+            halo_c[n, pl.ds(p * own, own), :] = jnp.where(grp > 0, halo_f[pl.ds(n * own, own), :], 0.0)
+
     for it in reversed(range(4)):
         s = 2 * it
-        before = halo_c[...] if it == 0 else start_row(s - 1)
+        before = halo_c[0] if it == 0 else start_row(s - 1)
         first, second = start_row(s), start_row(s + 1)
         now = change(jnp.concatenate([first, second], axis=1), jnp.concatenate([before, first], axis=1))
         for t in range(2):
             row = grp * 8 + s + t
             piece = jnp.where(row < live_rows, now[:, t * 128:(t + 1) * 128], 0.0)
             sec[:, pl.ds((s + t) * 128, 128)] = piece
-        if it == 3:
-            edge.start()
-
-    inflow = arrived(pick_out, picked_r)
-    inflow_s[...] = inflow
-    inflows = [to_pair(d, inflow_s, inflow_r.at[me_p], inflow_send, inflow_recv) for d in range(1, n_pair)]
-    for copy in inflows:
-        copy.start()
-    inflow_r[me_p] = inflow
-
-    for t in range(2):
-        cols = pl.ds(t * 128, 128)
-        v = ring[y, :, cols]
-        under = dens_rows[pl.ds(jnp.maximum(top_row - 1, 0) + t * own * height, own, stride=height), :]
-        prev = jnp.where(top_row == 0, inflow[:, t * 128:(t + 1) * 128], under)
-        ring2[y, :, cols] = v - own_cour * (v - prev) - own_rate * v
-    ring2_out = along_ring(ring2, ring2_send, ring2_recv)
+        if it == 2:
+            inflow, inflows, ring2_out = first_inflow()
+    edge[...] = change(halo_c[0], halo_c[1])
 
     def final_rows(it, before):
         v = sec[:, pl.ds(it * 256, 256)]
@@ -233,8 +235,7 @@
     biggest = None
     for it in reversed(range(4)):
         if it == 0:
-            edge.wait_recv()
-            before = edge_r[...]
+            before = edge[...]
         else:
             before = sec[:, pl.ds((2 * it - 1) * 128, 128)]
         for t, piece in enumerate(final_rows(it, before)):
@@ -307,9 +308,7 @@
         digits = out_r[p, pl.ds(own * 8, 32), :].astype(jnp.int32).astype(F32)[:own]
         scale = jnp.sum(digits * digit_size, axis=1, keepdims=True)
         tile = out_r[p, pl.ds(0, own * 8), :].astype(jnp.int32).astype(F32).reshape(own, 8, 128) * scale[:, :, None]
-        main_v[:, pl.ds((p // 2) * 8, 8), pl.ds((p % 2) * 128, 128)] = tile
-    store = pltpu.make_async_copy(main_v, main, local_sem.at[10])
-    store.start()
+        main[:, pl.ds((p // 2) * 8, 8), pl.ds((p % 2) * 128, 128)] = tile
 
     for q in range(2):
         @pl.when(me_p != q)
@@ -324,8 +323,7 @@
         top = linear[:, cols] + terms_s[pl.ds(me_p * own * 8 + t, own, stride=8), :]
         add_0[:, cols] += 0.5 * own_cour * top
 
-    store.wait()
-    for copy in (ring_out + main_in + pick_out + inflows + [edge] + outs + ring2_out + pick2_out):
+    for copy in (ring_out + main_in + pick_out + inflows + outs + ring2_out + pick2_out):
         copy.wait_send()
 
     @pl.when(grp == 0)
@@ -342,7 +340,7 @@
     vmem = pl.BlockSpec(memory_space=pltpu.VMEM)
     hbm = pl.BlockSpec(memory_space=pltpu.HBM)
     dma = pltpu.SemaphoreType.DMA
-    weight_rows = (2 * BANDS + 2) * piv + 16
+    weight_rows = (BANDS + 2) * piv + 16
     main, add_0, add_1 = pl.pallas_call(
         functools.partial(step_kernel, n_pair, own, piv, height, width),
         out_shape=(
@@ -351,7 +349,7 @@
             jax.ShapeDtypeStruct((own, width), F32),
         ),
         in_specs=[hbm] * 10,
-        out_specs=(hbm, vmem, vmem),
+        out_specs=(vmem, vmem, vmem),
         scratch_shapes=[
             pltpu.VMEM((piv, piv), F32),
             pltpu.VMEM((piv, piv), F32),
@@ -363,15 +361,14 @@
             pltpu.SMEM(upstream.shape, jnp.int32),
             pltpu.VMEM(face_map.shape, jnp.int32),
             pltpu.VMEM((2, own, height, 128), F32),
-            pltpu.VMEM((n_pair, own * 8 + 32, 128), I16),
-            pltpu.VMEM((n_pair, own * 8 + 32, 128), I16),
+            pltpu.VMEM((n_pair, own * 8 + 48, 128), I16),
+            pltpu.VMEM((n_pair, own * 8 + 48, 128), I16),
             pltpu.VMEM((piv * 8, 128), F32),
             pltpu.VMEM((piv, 1024), F32),
             pltpu.VMEM((piv, 1024), F32),
             pltpu.VMEM((piv * 8, 128), F32),
             pltpu.VMEM((n_pair, own * 8 + 32, 128), I16),
             pltpu.VMEM((n_pair, own * 8 + 32, 128), I16),
-            pltpu.VMEM((own, height, width), F32),
             pltpu.VMEM((weight_rows, piv), BF16),
             pltpu.VMEM((weight_rows, 256), F32),
             pltpu.VMEM((RING, own, width), F32),
@@ -380,8 +377,8 @@
             pltpu.VMEM((RING, own, width), F32),
             pltpu.VMEM((4, own, width), F32),
             pltpu.VMEM((4, own, width), F32),
-            pltpu.VMEM((32, 128), F32),
-            pltpu.VMEM((piv, 128), F32),
+            pltpu.VMEM((48, 128), F32),
+            pltpu.VMEM((2, piv, 128), F32),
             pltpu.VMEM((own, width), F32),
             pltpu.VMEM((n_pair, own, width), F32),
             pltpu.VMEM((piv, width), F32),
@@ -400,7 +397,6 @@
             dma((RING,)), dma((RING,)),
             dma((4,)), dma((4,)),
             dma((n_pair,)), dma((n_pair,)),
-            dma((n_pair,)), dma((n_pair,)),
         ],
         compiler_params=pltpu.CompilerParams(
             collective_id=0, has_side_effects=True, vmem_limit_bytes=56 * 1024 * 1024),

time: 31.8 us -> 31.7 us (level)
  no operation moved by 1% of the time
where the time goes in v7:
time: 31.7 us; the launch traced here: 31.6 us
  Pallas kernels  29.4 us (93%)
  other arithmetic  2.11 us (7%)
    pallas_call x1, Pallas kernels, shards(): pl.pallas_call(functools.partial(step_kernel, n_pair, own, piv, height, w...  29.4 us
    add x1, other arithmetic, shards(): main + jnp.where(row == 0, add_0[:, None, :], jnp.where(row == 1, add_1[:...  2.1 us

profile of v7, /device:TPU:1, one launch (start us, length us, event | category | flops | bytes accessed | tf_op | source)
XLA Modules:
  0.0 31.6 jit_solution(15430136462416204010)
XLA Ops:
  0.0 29.4 %shard_map.100 = (f32[20,32,256]{2,1,0:T(8,128)}, f32[20,256]{1,0:T(8,128)}, f32[20,256]{1,0:T(8,128)}) custom-call(f32[20,32,256]{2,1,0:T(8,128)} %density.1, f32[160,160]{1,0:T(8,128)} %agg_h.1, f32[160,160]{1,0:T(8,128)} %share_h.1, s32[160,160]{1,0:T(8,128)} %target_h.1, f32[160,160]{1,0:T(8,128)} %frag_h.1, f32[1,160]{1,0:T(1,128)} %bitcast.2, ...), custom_call_target="tpu_custom_call" | custom-call | tf_op jit(solution)/shard_map/pallas_call | solution.py:344
  29.4 2.1 %select_add_fusion = f32[20,32,256]{2,1,0:T(8,128)} fusion(f32[20,32,256]{2,1,0:T(8,128)} %get-tuple-element.8, f32[20,256]{1,0:T(8,128)} %get-tuple-element.10, f32[20,256]{1,0:T(8,128)} %get-tuple-element.9, pred[32]{0:T(512)(128)(4,1)S(1)} %get-tuple-element.11, pred[32]{0:T(512)(128)(4,1)S(1)} %get-tuple-element.12), kind=kLoop, calls=%fused_computation | loop fusion | flops 491520 | bytes 1351744 | tf_op jit(solution)/shard_map/add | solution.py:405
  (1 shorter events, 0.0 us)

commit v8 on v7

--- a/solution.py
+++ b/solution.py
@@ -344,9 +344,9 @@
     main, add_0, add_1 = pl.pallas_call(
         functools.partial(step_kernel, n_pair, own, piv, height, width),
         out_shape=(
-            jax.ShapeDtypeStruct(density.shape, F32),
-            jax.ShapeDtypeStruct((own, width), F32),
-            jax.ShapeDtypeStruct((own, width), F32),
+            pltpu.VMEM(density.shape, F32),
+            pltpu.VMEM((own, width), F32),
+            pltpu.VMEM((own, width), F32),
         ),
         in_specs=[hbm] * 10,
         out_specs=(vmem, vmem, vmem),

time: 31.7 us -> 29.6 us (0.934)
  other arithmetic: 2.11 us -> 1.02 us
  Pallas kernels: 29.4 us -> 28.5 us
    add x1, other arithmetic: 2.1 us -> 1.01 us  [shards(): main + jnp.where(row == 0, add_0[:, None, :], jnp.where(row == 1, add_1[:...]
    pallas_call x1, Pallas kernels: 29.4 us -> 28.5 us  [shards(): pl.pallas_call(functools.partial(step_kernel, n_pair, own, piv, height, w...]
where the time goes in v8:
time: 29.6 us; the launch traced here: 29.5 us
  Pallas kernels  28.5 us (96%)
  other arithmetic  1.02 us (3%)
    pallas_call x1, Pallas kernels, shards(): pl.pallas_call(functools.partial(step_kernel, n_pair, own, piv, height, w...  28.5 us
    add x1, other arithmetic, shards(): main + jnp.where(row == 0, add_0[:, None, :], jnp.where(row == 1, add_1[:...  1.01 us

profile of v8, /device:TPU:1, one launch (start us, length us, event | category | flops | bytes accessed | tf_op | source)
XLA Modules:
  0.0 29.5 jit_solution(4521486193979095568)
XLA Ops:
  0.0 28.5 %shard_map.100 = (f32[20,32,256]{2,1,0:T(8,128)S(1)}, f32[20,256]{1,0:T(8,128)S(1)}, f32[20,256]{1,0:T(8,128)S(1)}) custom-call(f32[20,32,256]{2,1,0:T(8,128)} %density.1, f32[160,160]{1,0:T(8,128)} %agg_h.1, f32[160,160]{1,0:T(8,128)} %share_h.1, s32[160,160]{1,0:T(8,128)} %target_h.1, f32[160,160]{1,0:T(8,128)} %frag_h.1, f32[1,160]{1,0:T(1,128)} %bitcast.2, ...), custom_call_target="tpu_custom_call" | custom-call | tf_op jit(solution)/shard_map/pallas_call | solution.py:344
  28.5 1.0 %select_add_fusion = f32[20,32,256]{2,1,0:T(8,128)} fusion(f32[20,32,256]{2,1,0:T(8,128)S(1)} %get-tuple-element.8, f32[20,256]{1,0:T(8,128)S(1)} %get-tuple-element.10, f32[20,256]{1,0:T(8,128)S(1)} %get-tuple-element.9, pred[32]{0:T(512)(128)(4,1)S(1)} %get-tuple-element.11, pred[32]{0:T(512)(128)(4,1)S(1)} %get-tuple-element.12), kind=kLoop, calls=%fused_computation | loop fusion | flops 491520 | bytes 1351744 | tf_op jit(solution)/shard_map/add | solution.py:405
  (1 shorter events, 0.0 us)

commit v9 on v8

--- a/solution.py
+++ b/solution.py
@@ -38,10 +38,10 @@
     density, agg_h, share_h, target_h, frag_h, rate_h, cour_h, rows_h, up_h, map_h,
     main, add_0, add_1,
     agg, share, target, frag, rate, cour, rows_sm, up_sm, face_map, dens_v, enc, got, v0, sec, res, out_f, out_s, out_r, wb, y_s,
-    ring, picked, picked_r, ring2, picked2, picked2_r,
+    ring, picked, picked_r, stage,
     halo_f, halo_c, inflow_s, inflow_r, face, terms_s, late_s, late_p, late_r, edge, wide_s,
     local_sem, main_send, main_recv, inflow_send, inflow_recv, late_send, late_recv,
-    ring_send, ring_recv, pick_send, pick_recv, ring2_send, ring2_recv, pick2_send, pick2_recv,
+    ring_send, ring_recv, pick_send, pick_recv,
     out_send, out_recv,
 ):
     me_b, me_p = lax.axis_index("blk"), lax.axis_index("pair")
@@ -67,11 +67,12 @@
         load.start()
     scalars = [pltpu.make_async_copy(rows_h, rows_sm, local_sem.at[11]),
                pltpu.make_async_copy(up_h, up_sm, local_sem.at[12])]
-    for load in scalars:
+    map_load = pltpu.make_async_copy(map_h, face_map, local_sem.at[8])
+    for load in scalars + [map_load]:
         load.start()
     tables = [pltpu.make_async_copy(src, dst, local_sem.at[2 + n]) for n, (src, dst) in enumerate(
         ((agg_h, agg), (share_h, share), (target_h, target), (frag_h, frag),
-         (rate_h, rate), (cour_h, cour), (map_h, face_map)))]
+         (rate_h, rate), (cour_h, cour)))]
     for load in tables:
         load.start()
 
@@ -85,43 +86,29 @@
             src_ref=src, dst_ref=dst, send_sem=send.at[d], recv_sem=recv.at[d],
             device_id=(b, me_p), device_id_type=MESH)
 
-    def along_ring(faces, send, recv):
-        copies = [to_block(ring_mates[d], d, faces.at[y], faces.at[y], send, recv) for d in range(1, RING)]
-        for copy in copies:
-            copy.start()
-        return copies
-
-    def across(faces, copies, chosen, chosen_r, send, recv):
-        for copy in copies:
-            copy.wait_recv()
-        for q in range(1, 4):
-            chosen[q] = faces[(up_sm[pick_mates[q]] // CORES) % RING]
-        more = [to_block(pick_mates[q], q, chosen.at[q], chosen_r.at[q], send, recv) for q in range(1, 4)]
-        for copy in more:
-            copy.start()
-        chosen_r[0] = faces[(up_sm[me_b] // CORES) % RING]
-        return more
-
-    def arrived(copies, chosen_r):
-        for copy in copies:
-            copy.wait_recv()
-        u = up_sm[me_b]
-        q = ((u // (RING * CORES) + z_hi) % 2) * 2 + (u + core) % 2
-        return permuted(chosen_r[q], one_hot)
+    def ring_slot(b):
+        return (b // CORES) % RING
 
     halo_f[...] = jnp.zeros(halo_f.shape, F32)
+    stage[...] = jnp.zeros(stage.shape, F32)
     for load in scalars:
         load.wait()
     live_rows = rows_sm[me_b]
-    top_row = live_rows - 1
+    map_load.wait()
+    stage[pl.ds(44, 1), :] = face_map[...].astype(F32)
     for load in loads:
         load.wait()
     dens_rows = dens_v.reshape(2 * own * height, 128)
-    for t in range(2):
-        ring[y, :, pl.ds(t * 128, 128)] = dens_rows[
-            pl.ds(jnp.maximum(top_row, 0) + t * own * height, own, stride=height), :]
+    for n in range(2):
+        for t in range(2):
+            here = jnp.maximum(live_rows - 1 - n, 0) + t * own * height
+            stage[pl.ds(24 * n, own), pl.ds(t * 128, 128)] = (
+                dens_rows[pl.ds(here, own, stride=height), :] - MIDDLE) * (1.0 / STEP)
+    ring[y] = rounded16(stage[...])
     pl.semaphore_wait(barrier, len(pairs) + len(ring_mates) + len(pick_mates) - 3)
-    ring_out = along_ring(ring, ring_send, ring_recv)
+    ring_out = [to_block(ring_mates[d], d, ring.at[y], ring.at[y], ring_send, ring_recv) for d in range(1, RING)]
+    for copy in ring_out:
+        copy.start()
 
     main_in = []
     for d in ORDER + (0,):
@@ -169,7 +156,16 @@
     own_rate = jnp.sum(jnp.where(own_diag, rate_row, 0.0), axis=1, keepdims=True)
     one_hot = (lax.broadcasted_iota(jnp.int32, (width, width), 0) == face_map[...]).astype(F32).astype(BF16)
 
-    pick_out = across(ring, ring_out, picked, picked_r, pick_send, pick_recv)
+    for copy in ring_out:
+        copy.wait_recv()
+    for q in range(4):
+        feeder = up_sm[pick_mates[q]]
+        goal = picked.at[q] if q else picked_r.at[0]
+        goal[pl.ds(0, 48), :] = ring[ring_slot(feeder)]
+        goal[pl.ds(48, 32), :] = ring[ring_slot(up_sm[feeder]), pl.ds(0, 32), :]
+    pick_out = [to_block(pick_mates[q], q, picked.at[q], picked_r.at[q], pick_send, pick_recv) for q in range(1, 4)]
+    for copy in pick_out:
+        copy.start()
 
     def mixed(v):
         y_s[:, :v.shape[1]] = jnp.dot(wb[...], v.astype(BF16), preferred_element_type=F32)
@@ -188,22 +184,27 @@
     def start_row(s):
         return v0[pl.ds(s, piv, stride=8), :]
 
+    def pick_slot(b):
+        return ((b // (RING * CORES) + z_hi) % 2) * 2 + (b + core) % CORES
+
     def first_inflow():
-        inflow = arrived(pick_out, picked_r)
+        for copy in pick_out:
+            copy.wait_recv()
+        feeder = up_sm[me_b]
+        stage[...] = picked_r[pick_slot(feeder), pl.ds(0, 48), :].astype(jnp.int32).astype(F32)
+        inflow = permuted(stage[pl.ds(0, 24), :], one_hot)[:own] * STEP + MIDDLE
         inflow_s[...] = inflow
-        inflows = [to_pair(d, inflow_s, inflow_r.at[me_p], inflow_send, inflow_recv) for d in range(1, n_pair)]
+        inflows = [to_pair(d, inflow_s, inflow_r.at[me_p], inflow_send, inflow_recv) for d in ORDER]
         for copy in inflows:
             copy.start()
         inflow_r[me_p] = inflow
 
-        for t in range(2):
-            cols = pl.ds(t * 128, 128)
-            v = ring[y, :, cols]
-            under = dens_rows[pl.ds(jnp.maximum(top_row - 1, 0) + t * own * height, own, stride=height), :]
-            prev = jnp.where(top_row == 0, inflow[:, t * 128:(t + 1) * 128], under)
-            ring2[y, :, cols] = v - own_cour * (v - prev) - own_rate * v
-        ring2_out = along_ring(ring2, ring2_send, ring2_recv)
-        return inflow, inflows, ring2_out
+        feeder_hot = (lax.broadcasted_iota(jnp.int32, (width, width), 0).astype(F32) == stage[pl.ds(44, 1), :])
+        fed = picked_r[pick_slot(up_sm[feeder]), pl.ds(48, 32), :].astype(jnp.int32).astype(F32)
+        fed = permuted(fed, feeder_hot.astype(F32).astype(BF16))
+        prev = jnp.where(rows_sm[feeder] == 1, fed[:24], stage[pl.ds(24, 24), :])
+        prev = permuted(prev, one_hot)[:own] * STEP + MIDDLE
+        return inflows, inflow - own_cour * (inflow - prev) - own_rate * inflow
 
     for copy in main_in:
         copy.wait_recv()
@@ -223,8 +224,6 @@
             row = grp * 8 + s + t
             piece = jnp.where(row < live_rows, now[:, t * 128:(t + 1) * 128], 0.0)
             sec[:, pl.ds((s + t) * 128, 128)] = piece
-        if it == 2:
-            inflow, inflows, ring2_out = first_inflow()
     edge[...] = change(halo_c[0], halo_c[1])
 
     def final_rows(it, before):
@@ -244,8 +243,6 @@
             res[:, pl.ds((2 * it + t) * 128, 128)] = piece
             size = jnp.abs(piece)
             biggest = size if biggest is None else jnp.maximum(biggest, size)
-
-    pick2_out = across(ring2, ring2_out, picked2, picked2_r, pick2_send, pick2_recv)
 
     biggest = jnp.max(biggest, axis=1, keepdims=True)
     finer = jnp.where(biggest > 0.0, 32767.0 / biggest, 0.0)
@@ -267,6 +264,8 @@
     out_own = pltpu.make_async_copy(out_s.at[me_p], out_r.at[me_p], local_sem.at[9])
     out_own.start()
 
+    inflows, linear = first_inflow()
+
     for copy in inflows:
         copy.wait_recv()
     for p in range(n_pair):
@@ -317,13 +316,12 @@
     for t, add in enumerate((add_0, add_1)):
         for q in range(2):
             add[:, pl.ds(q * 128, 128)] = late_r[q, :, pl.ds(t * 128, 128)]
-    linear = arrived(pick2_out, picked2_r)
     for t in range(2):
         cols = slice(t * 128, (t + 1) * 128)
         top = linear[:, cols] + terms_s[pl.ds(me_p * own * 8 + t, own, stride=8), :]
         add_0[:, cols] += 0.5 * own_cour * top
 
-    for copy in (ring_out + main_in + pick_out + inflows + outs + ring2_out + pick2_out):
+    for copy in (ring_out + main_in + pick_out + inflows + outs):
         copy.wait_send()
 
     @pl.when(grp == 0)
@@ -371,12 +369,10 @@
             pltpu.VMEM((n_pair, own * 8 + 32, 128), I16),
             pltpu.VMEM((weight_rows, piv), BF16),
             pltpu.VMEM((weight_rows, 256), F32),
-            pltpu.VMEM((RING, own, width), F32),
-            pltpu.VMEM((4, own, width), F32),
-            pltpu.VMEM((4, own, width), F32),
-            pltpu.VMEM((RING, own, width), F32),
-            pltpu.VMEM((4, own, width), F32),
-            pltpu.VMEM((4, own, width), F32),
+            pltpu.VMEM((RING, 48, width), I16),
+            pltpu.VMEM((4, 80, width), I16),
+            pltpu.VMEM((4, 80, width), I16),
+            pltpu.VMEM((48, width), F32),
             pltpu.VMEM((48, 128), F32),
             pltpu.VMEM((2, piv, 128), F32),
             pltpu.VMEM((own, width), F32),
@@ -394,8 +390,6 @@
             dma((n_pair,)), dma((2,)),
             dma((RING,)), dma((RING,)),
             dma((4,)), dma((4,)),
-            dma((RING,)), dma((RING,)),
-            dma((4,)), dma((4,)),
             dma((n_pair,)), dma((n_pair,)),
         ],
         compiler_params=pltpu.CompilerParams(

time: 29.6 us -> 29.9 us (1.010)
  the two profiles are of different devices: /device:TPU:1 before, /device:TPU:20 now
where the time goes in v9:
time: 29.9 us; the launch traced here: 29.8 us
  Pallas kernels  28.8 us (96%)
  other arithmetic  1.02 us (3%)
    pallas_call x1, Pallas kernels, shards(): pl.pallas_call(functools.partial(step_kernel, n_pair, own, piv, height, w...  28.8 us
    add x1, other arithmetic, shards(): main + jnp.where(row == 0, add_0[:, None, :], jnp.where(row == 1, add_1[:...  1.01 us

profile of v9, /device:TPU:20, one launch (start us, length us, event | category | flops | bytes accessed | tf_op | source)
XLA Modules:
  0.0 29.8 jit_solution(10545100472659981113)
XLA Ops:
  0.0 28.8 %shard_map.100 = (f32[20,32,256]{2,1,0:T(8,128)S(1)}, f32[20,256]{1,0:T(8,128)S(1)}, f32[20,256]{1,0:T(8,128)S(1)}) custom-call(f32[20,32,256]{2,1,0:T(8,128)} %density.1, f32[160,160]{1,0:T(8,128)} %agg_h.1, f32[160,160]{1,0:T(8,128)} %share_h.1, s32[160,160]{1,0:T(8,128)} %target_h.1, f32[160,160]{1,0:T(8,128)} %frag_h.1, f32[1,160]{1,0:T(1,128)} %bitcast.2, ...), custom_call_target="tpu_custom_call" | custom-call | tf_op jit(solution)/shard_map/pallas_call | solution.py:342
  28.8 1.0 %select_add_fusion = f32[20,32,256]{2,1,0:T(8,128)} fusion(f32[20,32,256]{2,1,0:T(8,128)S(1)} %get-tuple-element.8, f32[20,256]{1,0:T(8,128)S(1)} %get-tuple-element.10, f32[20,256]{1,0:T(8,128)S(1)} %get-tuple-element.9, pred[32]{0:T(512)(128)(4,1)S(1)} %get-tuple-element.11, pred[32]{0:T(512)(128)(4,1)S(1)} %get-tuple-element.12), kind=kLoop, calls=%fused_computation | loop fusion | flops 491520 | bytes 1351744 | tf_op jit(solution)/shard_map/add | solution.py:399
  (1 shorter events, 0.0 us)

commit v10 on v9

--- a/solution.py
+++ b/solution.py
@@ -39,13 +39,13 @@
     main, add_0, add_1,
     agg, share, target, frag, rate, cour, rows_sm, up_sm, face_map, dens_v, enc, got, v0, sec, res, out_f, out_s, out_r, wb, y_s,
     ring, picked, picked_r, stage,
-    halo_f, halo_c, inflow_s, inflow_r, face, terms_s, late_s, late_p, late_r, edge, wide_s,
-    local_sem, main_send, main_recv, inflow_send, inflow_recv, late_send, late_recv,
+    halo_f, row_f, row_c, halo_c, inflow_s, inflow_r, face, row_s, edge, wide_s,
+    local_sem, main_send, main_recv, inflow_send, inflow_recv,
     ring_send, ring_recv, pick_send, pick_recv,
     out_send, out_recv,
 ):
     me_b, me_p = lax.axis_index("blk"), lax.axis_index("pair")
-    grp, half = me_p // 2, me_p % 2
+    grp = me_p // 2
     z_hi, y, core = me_b // (RING * CORES), (me_b // CORES) % RING, me_b % CORES
     pairs = [(me_p + d) % n_pair for d in range(n_pair)]
 
@@ -90,6 +90,7 @@
         return (b // CORES) % RING
 
     halo_f[...] = jnp.zeros(halo_f.shape, F32)
+    row_f[...] = jnp.zeros(row_f.shape, F32)
     stage[...] = jnp.zeros(stage.shape, F32)
     for load in scalars:
         load.wait()
@@ -110,6 +111,9 @@
     for copy in ring_out:
         copy.start()
 
+    for t in range(2):
+        row_f[pl.ds(t * own, own), :] = dens_rows[pl.ds(t * own * height, own, stride=height), :]
+    row_16 = rounded16((row_f[...] - MIDDLE) * (1.0 / STEP))
     main_in = []
     for d in ORDER + (0,):
         p = pairs[d]
@@ -120,9 +124,21 @@
         goal = enc.at[d] if d else got.at[me_p]
         goal[pl.ds(0, own * 8), :] = rounded16((tile - MIDDLE) * (1.0 / STEP))
         goal[pl.ds(own * 8, 48), :] = rounded16((halo_f[...] - MIDDLE) * (1.0 / STEP))
+        goal[pl.ds(own * 8 + 48, 48), :] = row_16
         if d:
             main_in.append(to_pair(d, enc.at[d], got.at[me_p], main_send, main_recv))
             main_in[-1].start()
+
+    for copy in ring_out:
+        copy.wait_recv()
+    for q in range(4):
+        feeder = up_sm[pick_mates[q]]
+        goal = picked.at[q] if q else picked_r.at[0]
+        goal[pl.ds(0, 48), :] = ring[ring_slot(feeder)]
+        goal[pl.ds(48, 32), :] = ring[ring_slot(up_sm[feeder]), pl.ds(0, 32), :]
+    pick_out = [to_block(pick_mates[q], q, picked.at[q], picked_r.at[q], pick_send, pick_recv) for q in range(1, 4)]
+    for copy in pick_out:
+        copy.start()
 
     for load in tables:
         load.wait()
@@ -156,17 +172,6 @@
     own_rate = jnp.sum(jnp.where(own_diag, rate_row, 0.0), axis=1, keepdims=True)
     one_hot = (lax.broadcasted_iota(jnp.int32, (width, width), 0) == face_map[...]).astype(F32).astype(BF16)
 
-    for copy in ring_out:
-        copy.wait_recv()
-    for q in range(4):
-        feeder = up_sm[pick_mates[q]]
-        goal = picked.at[q] if q else picked_r.at[0]
-        goal[pl.ds(0, 48), :] = ring[ring_slot(feeder)]
-        goal[pl.ds(48, 32), :] = ring[ring_slot(up_sm[feeder]), pl.ds(0, 32), :]
-    pick_out = [to_block(pick_mates[q], q, picked.at[q], picked_r.at[q], pick_send, pick_recv) for q in range(1, 4)]
-    for copy in pick_out:
-        copy.start()
-
     def mixed(v):
         y_s[:, :v.shape[1]] = jnp.dot(wb[...], v.astype(BF16), preferred_element_type=F32)
         vb = v.astype(BF16).astype(F32)
@@ -212,6 +217,9 @@
         v0[pl.ds(p * own * 8, own * 8), :] = (
             got[p, pl.ds(0, own * 8), :].astype(jnp.int32).astype(F32) * STEP + MIDDLE)
         halo_f[...] = got[p, pl.ds(own * 8, 48), :].astype(jnp.int32).astype(F32) * STEP + MIDDLE
+        row_f[...] = got[p, pl.ds(own * 8 + 48, 48), :].astype(jnp.int32).astype(F32) * STEP + MIDDLE
+        for t in range(2):
+            row_c[pl.ds(p * own, own), pl.ds(t * 128, 128)] = row_f[pl.ds(t * own, own), :]
         for n in range(2):
             halo_c[n, pl.ds(p * own, own), :] = jnp.where(grp > 0, halo_f[pl.ds(n * own, own), :], 0.0)
 
@@ -239,11 +247,12 @@
             before = sec[:, pl.ds((2 * it - 1) * 128, 128)]
         for t, piece in enumerate(final_rows(it, before)):
             row = grp * 8 + 2 * it + t
-            piece = jnp.where((row < live_rows) & (row >= 2), piece, 0.0)
+            piece = jnp.where((row < live_rows) & (row >= 1), piece, 0.0)
             res[:, pl.ds((2 * it + t) * 128, 128)] = piece
             size = jnp.abs(piece)
             biggest = size if biggest is None else jnp.maximum(biggest, size)
 
+    inflows, linear = first_inflow()
     biggest = jnp.max(biggest, axis=1, keepdims=True)
     finer = jnp.where(biggest > 0.0, 32767.0 / biggest, 0.0)
     for s in range(8):
@@ -264,37 +273,24 @@
     out_own = pltpu.make_async_copy(out_s.at[me_p], out_r.at[me_p], local_sem.at[9])
     out_own.start()
 
-    inflows, linear = first_inflow()
 
     for copy in inflows:
         copy.wait_recv()
     for p in range(n_pair):
         face[pl.ds(p * own, own), :] = inflow_r[p]
 
-    def late_copy(p, source):
-        return pltpu.make_async_remote_copy(
-            src_ref=late_p.at[p], dst_ref=late_r.at[source], send_sem=late_send.at[p],
-            recv_sem=late_recv.at[source], device_id=(me_b, p), device_id_type=MESH)
-
-    @pl.when(grp == 0)
-    def _():
-        sec[:, :128] += cour_col * jnp.where(half == 0, face[:, :128], face[:, 128:])
-        for t, piece in enumerate(final_rows(0, jnp.zeros((piv, 128), F32))):
-            late_s[:, pl.ds(t * 128, 128)] = jnp.where(t < live_rows, piece, 0.0)
-        for p in range(n_pair):
-            late_p[p] = late_s[pl.ds(p * own, own), :]
-        for p in range(n_pair):
-            @pl.when(me_p != p)
-            def _():
-                late_copy(p, me_p).start()
-
-            @pl.when(me_p == p)
-            def _():
-                late_r[min(p, 1)] = late_p[p]
-
-    terms = mixed(face[...])
+    inflow_all = face[...]
+    start = row_c[...]
+    moved = change(start, inflow_all)
+    row_0 = 0.5 * start + 0.5 * (moved + (mixed(moved) - rate_col * moved - cour_col * moved))
+    row_0 = row_0 + 0.5 * cour_col * mixed(inflow_all)
     for t in range(2):
-        terms_s[pl.ds(t, piv, stride=8), :] = terms[:, t * 128:(t + 1) * 128]
+        row_s[pl.ds(t, piv, stride=8), :] = row_0[:, t * 128:(t + 1) * 128]
+    for t in range(2):
+        cols = slice(t * 128, (t + 1) * 128)
+        mine = row_s[pl.ds(me_p * own * 8 + t, own, stride=8), :]
+        add_0[:, cols] = mine + 0.5 * own_cour * linear[:, cols]
+        add_1[:, cols] = jnp.where(live_rows > 1, 0.5 * own_cour * own_cour * inflow_s[:, cols], 0.0)
 
     digit = lax.broadcasted_iota(jnp.int32, (own, 128), 1)
     digit_size = jnp.where(
@@ -309,27 +305,8 @@
         tile = out_r[p, pl.ds(0, own * 8), :].astype(jnp.int32).astype(F32).reshape(own, 8, 128) * scale[:, :, None]
         main[:, pl.ds((p // 2) * 8, 8), pl.ds((p % 2) * 128, 128)] = tile
 
-    for q in range(2):
-        @pl.when(me_p != q)
-        def _():
-            late_copy(0, q).wait_recv()
-    for t, add in enumerate((add_0, add_1)):
-        for q in range(2):
-            add[:, pl.ds(q * 128, 128)] = late_r[q, :, pl.ds(t * 128, 128)]
-    for t in range(2):
-        cols = slice(t * 128, (t + 1) * 128)
-        top = linear[:, cols] + terms_s[pl.ds(me_p * own * 8 + t, own, stride=8), :]
-        add_0[:, cols] += 0.5 * own_cour * top
-
     for copy in (ring_out + main_in + pick_out + inflows + outs):
         copy.wait_send()
-
-    @pl.when(grp == 0)
-    def _():
-        for p in range(n_pair):
-            @pl.when(me_p != p)
-            def _():
-                late_copy(p, me_p).wait_send()
 
 
 def shards(n_pair, density, agg, share, target, frag, rate, cour, block_rows, upstream, face_map):
@@ -359,8 +336,8 @@
             pltpu.SMEM(upstream.shape, jnp.int32),
             pltpu.VMEM(face_map.shape, jnp.int32),
             pltpu.VMEM((2, own, height, 128), F32),
-            pltpu.VMEM((n_pair, own * 8 + 48, 128), I16),
-            pltpu.VMEM((n_pair, own * 8 + 48, 128), I16),
+            pltpu.VMEM((n_pair, own * 8 + 96, 128), I16),
+            pltpu.VMEM((n_pair, own * 8 + 96, 128), I16),
             pltpu.VMEM((piv * 8, 128), F32),
             pltpu.VMEM((piv, 1024), F32),
             pltpu.VMEM((piv, 1024), F32),
@@ -374,20 +351,18 @@
             pltpu.VMEM((4, 80, width), I16),
             pltpu.VMEM((48, width), F32),
             pltpu.VMEM((48, 128), F32),
+            pltpu.VMEM((48, 128), F32),
+            pltpu.VMEM((piv, width), F32),
             pltpu.VMEM((2, piv, 128), F32),
             pltpu.VMEM((own, width), F32),
             pltpu.VMEM((n_pair, own, width), F32),
             pltpu.VMEM((piv, width), F32),
             pltpu.VMEM((piv * 8, 128), F32),
-            pltpu.VMEM((piv, 256), F32),
-            pltpu.VMEM((n_pair, own, 256), F32),
-            pltpu.VMEM((2, own, 256), F32),
             pltpu.VMEM((piv, 128), F32),
             pltpu.VMEM((piv + 16, 128), F32),
             dma((13,)),
             dma((n_pair,)), dma((n_pair,)),
             dma((n_pair,)), dma((n_pair,)),
-            dma((n_pair,)), dma((2,)),
             dma((RING,)), dma((RING,)),
             dma((4,)), dma((4,)),
             dma((n_pair,)), dma((n_pair,)),

time: 29.9 us -> 27.7 us (0.926)
  the two profiles are of different devices: /device:TPU:20 before, /device:TPU:1 now
where the time goes in v10:
time: 27.7 us; the launch traced here: 27.6 us
  Pallas kernels  26.6 us (96%)
  other arithmetic  1.02 us (4%)
    pallas_call x1, Pallas kernels, shards(): pl.pallas_call(functools.partial(step_kernel, n_pair, own, piv, height, w...  26.6 us
    add x1, other arithmetic, shards(): main + jnp.where(row == 0, add_0[:, None, :], jnp.where(row == 1, add_1[:...  1.01 us

profile of v10, /device:TPU:1, one launch (start us, length us, event | category | flops | bytes accessed | tf_op | source)
XLA Modules:
  0.0 27.6 jit_solution(4864560223308212296)
XLA Ops:
  0.0 26.6 %shard_map.100 = (f32[20,32,256]{2,1,0:T(8,128)S(1)}, f32[20,256]{1,0:T(8,128)S(1)}, f32[20,256]{1,0:T(8,128)S(1)}) custom-call(f32[20,32,256]{2,1,0:T(8,128)} %density.1, f32[160,160]{1,0:T(8,128)} %agg_h.1, f32[160,160]{1,0:T(8,128)} %share_h.1, s32[160,160]{1,0:T(8,128)} %target_h.1, f32[160,160]{1,0:T(8,128)} %frag_h.1, f32[1,160]{1,0:T(1,128)} %bitcast.2, ...), custom_call_target="tpu_custom_call" | custom-call | tf_op jit(solution)/shard_map/pallas_call | solution.py:319
  26.6 1.0 %select_add_fusion = f32[20,32,256]{2,1,0:T(8,128)} fusion(f32[20,32,256]{2,1,0:T(8,128)S(1)} %get-tuple-element.8, f32[20,256]{1,0:T(8,128)S(1)} %get-tuple-element.10, f32[20,256]{1,0:T(8,128)S(1)} %get-tuple-element.9, pred[32]{0:T(512)(128)(4,1)S(1)} %get-tuple-element.11, pred[32]{0:T(512)(128)(4,1)S(1)} %get-tuple-element.12), kind=kLoop, calls=%fused_computation | loop fusion | flops 491520 | bytes 1351744 | tf_op jit(solution)/shard_map/add | solution.py:374
  (1 shorter events, 0.0 us)

commit v11 on v10

--- a/solution.py
+++ b/solution.py
@@ -39,7 +39,7 @@
     main, add_0, add_1,
     agg, share, target, frag, rate, cour, rows_sm, up_sm, face_map, dens_v, enc, got, v0, sec, res, out_f, out_s, out_r, wb, y_s,
     ring, picked, picked_r, stage,
-    halo_f, row_f, row_c, halo_c, inflow_s, inflow_r, face, row_s, edge, wide_s,
+    side, row_c, halo_c, inflow_f, inflow_s, inflow_r, face, row_s, edge, wide_s,
     local_sem, main_send, main_recv, inflow_send, inflow_recv,
     ring_send, ring_recv, pick_send, pick_recv,
     out_send, out_recv,
@@ -89,8 +89,7 @@
     def ring_slot(b):
         return (b // CORES) % RING
 
-    halo_f[...] = jnp.zeros(halo_f.shape, F32)
-    row_f[...] = jnp.zeros(row_f.shape, F32)
+    inflow_f[...] = jnp.zeros(inflow_f.shape, F32)
     stage[...] = jnp.zeros(stage.shape, F32)
     for load in scalars:
         load.wait()
@@ -112,19 +111,17 @@
         copy.start()
 
     for t in range(2):
-        row_f[pl.ds(t * own, own), :] = dens_rows[pl.ds(t * own * height, own, stride=height), :]
-    row_16 = rounded16((row_f[...] - MIDDLE) * (1.0 / STEP))
+        side[pl.ds((2 + t) * own, own), :] = dens_rows[pl.ds(t * own * height, own, stride=height), :]
     main_in = []
     for d in ORDER + (0,):
         p = pairs[d]
         tile = dens_v[p % 2, :, pl.ds(pl.multiple_of((p // 2) * 8, 8), 8), :].reshape(own * 8, 128)
         for n in range(2):
             under = jnp.maximum((p // 2) * 8 - 1 - n, 0) + (p % 2) * own * height
-            halo_f[pl.ds(n * own, own), :] = dens_rows[pl.ds(under, own, stride=height), :]
+            side[pl.ds(n * own, own), :] = dens_rows[pl.ds(under, own, stride=height), :]
         goal = enc.at[d] if d else got.at[me_p]
         goal[pl.ds(0, own * 8), :] = rounded16((tile - MIDDLE) * (1.0 / STEP))
-        goal[pl.ds(own * 8, 48), :] = rounded16((halo_f[...] - MIDDLE) * (1.0 / STEP))
-        goal[pl.ds(own * 8 + 48, 48), :] = row_16
+        goal[pl.ds(own * 8, own * 4), :] = rounded16((side[...] - MIDDLE) * (1.0 / STEP))
         if d:
             main_in.append(to_pair(d, enc.at[d], got.at[me_p], main_send, main_recv))
             main_in[-1].start()
@@ -197,31 +194,33 @@
             copy.wait_recv()
         feeder = up_sm[me_b]
         stage[...] = picked_r[pick_slot(feeder), pl.ds(0, 48), :].astype(jnp.int32).astype(F32)
-        inflow = permuted(stage[pl.ds(0, 24), :], one_hot)[:own] * STEP + MIDDLE
-        inflow_s[...] = inflow
+        steps = permuted(stage[pl.ds(0, 24), :], one_hot)[:own]
+        for t in range(2):
+            inflow_f[pl.ds(t * own, own), :] = steps[:, t * 128:(t + 1) * 128]
+        inflow_s[...] = rounded16(inflow_f[...])
         inflows = [to_pair(d, inflow_s, inflow_r.at[me_p], inflow_send, inflow_recv) for d in ORDER]
         for copy in inflows:
             copy.start()
-        inflow_r[me_p] = inflow
+        inflow_r[me_p] = inflow_s[...]
+        inflow = steps * STEP + MIDDLE
 
         feeder_hot = (lax.broadcasted_iota(jnp.int32, (width, width), 0).astype(F32) == stage[pl.ds(44, 1), :])
         fed = picked_r[pick_slot(up_sm[feeder]), pl.ds(48, 32), :].astype(jnp.int32).astype(F32)
         fed = permuted(fed, feeder_hot.astype(F32).astype(BF16))
         prev = jnp.where(rows_sm[feeder] == 1, fed[:24], stage[pl.ds(24, 24), :])
         prev = permuted(prev, one_hot)[:own] * STEP + MIDDLE
-        return inflows, inflow - own_cour * (inflow - prev) - own_rate * inflow
+        return inflows, inflow, inflow - own_cour * (inflow - prev) - own_rate * inflow
 
     for copy in main_in:
         copy.wait_recv()
     for p in range(n_pair):
         v0[pl.ds(p * own * 8, own * 8), :] = (
             got[p, pl.ds(0, own * 8), :].astype(jnp.int32).astype(F32) * STEP + MIDDLE)
-        halo_f[...] = got[p, pl.ds(own * 8, 48), :].astype(jnp.int32).astype(F32) * STEP + MIDDLE
-        row_f[...] = got[p, pl.ds(own * 8 + 48, 48), :].astype(jnp.int32).astype(F32) * STEP + MIDDLE
-        for t in range(2):
-            row_c[pl.ds(p * own, own), pl.ds(t * 128, 128)] = row_f[pl.ds(t * own, own), :]
+        side[...] = got[p, pl.ds(own * 8, own * 4), :].astype(jnp.int32).astype(F32) * STEP + MIDDLE
+        for t in range(2):
+            row_c[pl.ds(p * own, own), pl.ds(t * 128, 128)] = side[pl.ds((2 + t) * own, own), :]
         for n in range(2):
-            halo_c[n, pl.ds(p * own, own), :] = jnp.where(grp > 0, halo_f[pl.ds(n * own, own), :], 0.0)
+            halo_c[n, pl.ds(p * own, own), :] = jnp.where(grp > 0, side[pl.ds(n * own, own), :], 0.0)
 
     for it in reversed(range(4)):
         s = 2 * it
@@ -252,7 +251,7 @@
             size = jnp.abs(piece)
             biggest = size if biggest is None else jnp.maximum(biggest, size)
 
-    inflows, linear = first_inflow()
+    inflows, inflow, linear = first_inflow()
     biggest = jnp.max(biggest, axis=1, keepdims=True)
     finer = jnp.where(biggest > 0.0, 32767.0 / biggest, 0.0)
     for s in range(8):
@@ -277,7 +276,9 @@
     for copy in inflows:
         copy.wait_recv()
     for p in range(n_pair):
-        face[pl.ds(p * own, own), :] = inflow_r[p]
+        inflow_f[...] = inflow_r[p].astype(jnp.int32).astype(F32) * STEP + MIDDLE
+        for t in range(2):
+            face[pl.ds(p * own, own), pl.ds(t * 128, 128)] = inflow_f[pl.ds(t * own, own), :]
 
     inflow_all = face[...]
     start = row_c[...]
@@ -290,7 +291,7 @@
         cols = slice(t * 128, (t + 1) * 128)
         mine = row_s[pl.ds(me_p * own * 8 + t, own, stride=8), :]
         add_0[:, cols] = mine + 0.5 * own_cour * linear[:, cols]
-        add_1[:, cols] = jnp.where(live_rows > 1, 0.5 * own_cour * own_cour * inflow_s[:, cols], 0.0)
+        add_1[:, cols] = jnp.where(live_rows > 1, 0.5 * own_cour * own_cour * inflow[:, cols], 0.0)
 
     digit = lax.broadcasted_iota(jnp.int32, (own, 128), 1)
     digit_size = jnp.where(
@@ -336,8 +337,8 @@
             pltpu.SMEM(upstream.shape, jnp.int32),
             pltpu.VMEM(face_map.shape, jnp.int32),
             pltpu.VMEM((2, own, height, 128), F32),
-            pltpu.VMEM((n_pair, own * 8 + 96, 128), I16),
-            pltpu.VMEM((n_pair, own * 8 + 96, 128), I16),
+            pltpu.VMEM((n_pair, own * 12, 128), I16),
+            pltpu.VMEM((n_pair, own * 12, 128), I16),
             pltpu.VMEM((piv * 8, 128), F32),
             pltpu.VMEM((piv, 1024), F32),
             pltpu.VMEM((piv, 1024), F32),
@@ -350,12 +351,12 @@
             pltpu.VMEM((4, 80, width), I16),
             pltpu.VMEM((4, 80, width), I16),
             pltpu.VMEM((48, width), F32),
-            pltpu.VMEM((48, 128), F32),
-            pltpu.VMEM((48, 128), F32),
+            pltpu.VMEM((own * 4, 128), F32),
             pltpu.VMEM((piv, width), F32),
             pltpu.VMEM((2, piv, 128), F32),
-            pltpu.VMEM((own, width), F32),
-            pltpu.VMEM((n_pair, own, width), F32),
+            pltpu.VMEM((48, 128), F32),
+            pltpu.VMEM((48, 128), I16),
+            pltpu.VMEM((n_pair, 48, 128), I16),
             pltpu.VMEM((piv, width), F32),
             pltpu.VMEM((piv * 8, 128), F32),
             pltpu.VMEM((piv, 128), F32),

time: 27.7 us -> 27.1 us (0.978)
  Pallas kernels: 26.6 us -> 25.9 us
    pallas_call x1, Pallas kernels: 26.6 us -> 25.9 us  [shards(): pl.pallas_call(functools.partial(step_kernel, n_pair, own, piv, height, w...]
where the time goes in v11:
time: 27.1 us; the launch traced here: 27 us
  Pallas kernels  25.9 us (96%)
  other arithmetic  1.02 us (4%)
    pallas_call x1, Pallas kernels, shards(): pl.pallas_call(functools.partial(step_kernel, n_pair, own, piv, height, w...  25.9 us
    add x1, other arithmetic, shards(): main + jnp.where(row == 0, add_0[:, None, :], jnp.where(row == 1, add_1[:...  1.01 us

profile of v11, /device:TPU:1, one launch (start us, length us, event | category | flops | bytes accessed | tf_op | source)
XLA Modules:
  0.0 27.0 jit_solution(6598916665654230760)
XLA Ops:
  0.0 25.9 %shard_map.100 = (f32[20,32,256]{2,1,0:T(8,128)S(1)}, f32[20,256]{1,0:T(8,128)S(1)}, f32[20,256]{1,0:T(8,128)S(1)}) custom-call(f32[20,32,256]{2,1,0:T(8,128)} %density.1, f32[160,160]{1,0:T(8,128)} %agg_h.1, f32[160,160]{1,0:T(8,128)} %share_h.1, s32[160,160]{1,0:T(8,128)} %target_h.1, f32[160,160]{1,0:T(8,128)} %frag_h.1, f32[1,160]{1,0:T(1,128)} %bitcast.2, ...), custom_call_target="tpu_custom_call" | custom-call | tf_op jit(solution)/shard_map/pallas_call | solution.py:320
  26.0 1.0 %select_add_fusion = f32[20,32,256]{2,1,0:T(8,128)} fusion(f32[20,32,256]{2,1,0:T(8,128)S(1)} %get-tuple-element.8, f32[20,256]{1,0:T(8,128)S(1)} %get-tuple-element.10, f32[20,256]{1,0:T(8,128)S(1)} %get-tuple-element.9, pred[32]{0:T(512)(128)(4,1)S(1)} %get-tuple-element.11, pred[32]{0:T(512)(128)(4,1)S(1)} %get-tuple-element.12), kind=kLoop, calls=%fused_computation | loop fusion | flops 491520 | bytes 1351744 | tf_op jit(solution)/shard_map/add | solution.py:375
  (1 shorter events, 0.0 us)

commit v12 on v11

--- a/solution.py
+++ b/solution.py
@@ -13,7 +13,7 @@
 BF16 = jnp.bfloat16
 I16 = jnp.int16
 RING, CORES = 4, 2
-ORDER = (4, 3, 5, 2, 6, 1, 7)
+ORDER = (1, 7, 2, 6, 3, 5, 4)
 MIDDLE = 1.025
 STEP = 1.95 / 65534.0
 LEAST = 32768.0 / 65536.0

time: 27.1 us -> 26.6 us (0.982)
  Pallas kernels: 25.9 us -> 25.4 us
    pallas_call x1, Pallas kernels: 25.9 us -> 25.4 us  [shards(): pl.pallas_call(functools.partial(step_kernel, n_pair, own, piv, height, w...]
where the time goes in v12:
time: 26.6 us; the launch traced here: 26.5 us
  Pallas kernels  25.4 us (95%)
  other arithmetic  1.02 us (4%)
    pallas_call x1, Pallas kernels, shards(): pl.pallas_call(functools.partial(step_kernel, n_pair, own, piv, height, w...  25.4 us
    add x1, other arithmetic, shards(): main + jnp.where(row == 0, add_0[:, None, :], jnp.where(row == 1, add_1[:...  1.01 us

profile of v12, /device:TPU:1, one launch (start us, length us, event | category | flops | bytes accessed | tf_op | source)
XLA Modules:
  0.0 26.5 jit_solution(13489735015008228872)
XLA Ops:
  0.0 25.4 %shard_map.100 = (f32[20,32,256]{2,1,0:T(8,128)S(1)}, f32[20,256]{1,0:T(8,128)S(1)}, f32[20,256]{1,0:T(8,128)S(1)}) custom-call(f32[20,32,256]{2,1,0:T(8,128)} %density.1, f32[160,160]{1,0:T(8,128)} %agg_h.1, f32[160,160]{1,0:T(8,128)} %share_h.1, s32[160,160]{1,0:T(8,128)} %target_h.1, f32[160,160]{1,0:T(8,128)} %frag_h.1, f32[1,160]{1,0:T(1,128)} %bitcast.2, ...), custom_call_target="tpu_custom_call" | custom-call | tf_op jit(solution)/shard_map/pallas_call | solution.py:320
  25.5 1.0 %select_add_fusion = f32[20,32,256]{2,1,0:T(8,128)} fusion(f32[20,32,256]{2,1,0:T(8,128)S(1)} %get-tuple-element.8, f32[20,256]{1,0:T(8,128)S(1)} %get-tuple-element.10, f32[20,256]{1,0:T(8,128)S(1)} %get-tuple-element.9, pred[32]{0:T(512)(128)(4,1)S(1)} %get-tuple-element.11, pred[32]{0:T(512)(128)(4,1)S(1)} %get-tuple-element.12), kind=kLoop, calls=%fused_computation | loop fusion | flops 491520 | bytes 1351744 | tf_op jit(solution)/shard_map/add | solution.py:375
  (1 shorter events, 0.0 us)

commit v13 on v12

--- a/solution.py
+++ b/solution.py
@@ -202,14 +202,16 @@
         for copy in inflows:
             copy.start()
         inflow_r[me_p] = inflow_s[...]
-        inflow = steps * STEP + MIDDLE
-
+        return inflows, steps * STEP + MIDDLE
+
+    def linear_part(inflow):
+        feeder = up_sm[me_b]
         feeder_hot = (lax.broadcasted_iota(jnp.int32, (width, width), 0).astype(F32) == stage[pl.ds(44, 1), :])
         fed = picked_r[pick_slot(up_sm[feeder]), pl.ds(48, 32), :].astype(jnp.int32).astype(F32)
         fed = permuted(fed, feeder_hot.astype(F32).astype(BF16))
         prev = jnp.where(rows_sm[feeder] == 1, fed[:24], stage[pl.ds(24, 24), :])
         prev = permuted(prev, one_hot)[:own] * STEP + MIDDLE
-        return inflows, inflow, inflow - own_cour * (inflow - prev) - own_rate * inflow
+        return inflow - own_cour * (inflow - prev) - own_rate * inflow
 
     for copy in main_in:
         copy.wait_recv()
@@ -251,7 +253,7 @@
             size = jnp.abs(piece)
             biggest = size if biggest is None else jnp.maximum(biggest, size)
 
-    inflows, inflow, linear = first_inflow()
+    inflows, inflow = first_inflow()
     biggest = jnp.max(biggest, axis=1, keepdims=True)
     finer = jnp.where(biggest > 0.0, 32767.0 / biggest, 0.0)
     for s in range(8):
@@ -271,6 +273,7 @@
         copy.start()
     out_own = pltpu.make_async_copy(out_s.at[me_p], out_r.at[me_p], local_sem.at[9])
     out_own.start()
+    linear = linear_part(inflow)
 
 
     for copy in inflows:

time: 26.6 us -> 26.6 us (level)
  no operation moved by 1% of the time
where the time goes in v13:
time: 26.6 us; the launch traced here: 26.5 us
  Pallas kernels  25.5 us (96%)
  other arithmetic  1.02 us (4%)
    pallas_call x1, Pallas kernels, shards(): pl.pallas_call(functools.partial(step_kernel, n_pair, own, piv, height, w...  25.5 us
    add x1, other arithmetic, shards(): main + jnp.where(row == 0, add_0[:, None, :], jnp.where(row == 1, add_1[:...  1.01 us

profile of v13, /device:TPU:1, one launch (start us, length us, event | category | flops | bytes accessed | tf_op | source)
XLA Modules:
  0.0 26.5 jit_solution(17623952980210947206)
XLA Ops:
  0.0 25.5 %shard_map.100 = (f32[20,32,256]{2,1,0:T(8,128)S(1)}, f32[20,256]{1,0:T(8,128)S(1)}, f32[20,256]{1,0:T(8,128)S(1)}) custom-call(f32[20,32,256]{2,1,0:T(8,128)} %density.1, f32[160,160]{1,0:T(8,128)} %agg_h.1, f32[160,160]{1,0:T(8,128)} %share_h.1, s32[160,160]{1,0:T(8,128)} %target_h.1, f32[160,160]{1,0:T(8,128)} %frag_h.1, f32[1,160]{1,0:T(1,128)} %bitcast.2, ...), custom_call_target="tpu_custom_call" | custom-call | tf_op jit(solution)/shard_map/pallas_call | solution.py:323
  25.5 1.0 %select_add_fusion = f32[20,32,256]{2,1,0:T(8,128)} fusion(f32[20,32,256]{2,1,0:T(8,128)S(1)} %get-tuple-element.8, f32[20,256]{1,0:T(8,128)S(1)} %get-tuple-element.10, f32[20,256]{1,0:T(8,128)S(1)} %get-tuple-element.9, pred[32]{0:T(512)(128)(4,1)S(1)} %get-tuple-element.11, pred[32]{0:T(512)(128)(4,1)S(1)} %get-tuple-element.12), kind=kLoop, calls=%fused_computation | loop fusion | flops 491520 | bytes 1351744 | tf_op jit(solution)/shard_map/add | solution.py:378
  (1 shorter events, 0.0 us)
